TPU v7x, 32 devices: a whole 2x2x4 slice. The times are simulated.
32 devices in a mesh: member: 4 (over z), band: 8 (over y, x, core).
Axes of the slice: x: 2, y: 2, z: 4, core: 2. Of those that a mesh axis runs over, the one named last changes fastest.
Arguments:
- latent: bfloat16 [4, 2048, 1024], P('member', 'band'), may hold values from -6 to 6
- observed: bfloat16 [2048, 128], P('band'), may hold values from -6 to 6
- area_weight: float32 [2048], P('band'), may hold values from 0.3 to 25, as said below
- band_counts: int32 [8], replicated, may hold values from 128 to 256, as said below
- gain_attn: float32 [1024], replicated, may hold values from 0.25 to 1.75
- w_query: bfloat16 [1024, 1024], replicated, may hold values from -0.1875 to 0.1875
- w_key: bfloat16 [1024, 1024], replicated, may hold values from -0.1875 to 0.1875
- w_value: bfloat16 [1024, 1024], replicated, may hold values from -0.1875 to 0.1875
- w_out: bfloat16 [1024, 1024], replicated, may hold values from -1.5 to 1.5
- gain_head: float32 [1024], replicated, may hold values from 0.25 to 1.75
- w_head: bfloat16 [1024, 128], replicated, may hold values from -0.1875 to 0.1875
Outputs:
- grad_latent: bfloat16 [4, 2048, 1024], P('member', 'band')
- grad_head: float32 [1024, 128], P('band')
- ensemble_loss: float32 [], replicated
Inputs may be any that keep to these rules, and one draw needn't show every extreme that they name: Band b holds band_counts[b] live grid points in its first slots; the remaining of its 256 slots are padding. In every draw some band holds exactly 256 and another exactly 128. `area_weight`: positive area weights.
All inputs are finite; a program needn't handle non-finite values.
Results may differ from a plain program's by a relative error of at most 0.019.
Values may be sent and summed in bfloat16 or wider, within the bound.
A program may use at most 192 MiB of HBM per device.

v0:
```python
import math

import jax
import jax.numpy as jnp
from jax import lax
from jax.sharding import PartitionSpec as P

HEADS = 16
CH = 128
R = 512
HOPS = 4


NORM_EPS = 1e-06
SMOOTH_WIDTH = 0.25
FAIR_ALPHA = 0.95
heads_per_group = 4


def from_behind(value, axis, steps):
    count = lax.axis_size(axis)
    leading, last = (max(0, -steps), min(count, count - steps))
    return lax.ppermute(value, axis, [(source, source + steps) for source in range(leading, last)])


def inverse_rms(values):
    return lax.rsqrt(jnp.mean(values * values, axis=-1, keepdims=True) + NORM_EPS)


def norm_backward(values, gain_vec, inverse, upstream):
    scaled = upstream * gain_vec
    return inverse * scaled - values * inverse**3 * jnp.mean(
        values * scaled, axis=-1, keepdims=True
    )


def times_transposed(left_side, scaling_coefficient):
    return lax.dot_general(
        left_side,
        scaling_coefficient,
        (((left_side.ndim - 1,), (1,)), ((), ())),
        preferred_element_type=jnp.float32,
    )


def window_probs(query_group, key_group, allowed):
    head_size = query_group.shape[-1]
    scores = jnp.einsum(
        "mqgd,mkgd->mgqk", query_group, key_group, preferred_element_type=jnp.float32
    ) * (1.0 / math.sqrt(head_size))
    exponent = jnp.where(allowed[None, None], jnp.exp(scores), 0.0)
    return exponent / jnp.sum(exponent, axis=-1, keepdims=True)


def split_group(array_in, first_col, group_width, head_size):
    part_cols = lax.dynamic_slice_in_dim(array_in, first_col, group_width, 2)
    return part_cols.reshape(array_in.shape[0], array_in.shape[1], heads_per_group, head_size)


def attention_forward(queries, key_rows, value_rows, allowed):
    number_of_realizations, row_count, model_width = queries.shape
    head_size = model_width // HEADS
    group_width = heads_per_group * head_size

    def one_group(group_index, output):
        first_col = (group_index * group_width).astype(jnp.int32)
        query_group = split_group(queries, first_col, group_width, head_size)
        key_group = split_group(key_rows, first_col, group_width, head_size)
        value_group = split_group(value_rows, first_col, group_width, head_size)
        soft_b = window_probs(query_group, key_group, allowed).astype(jnp.bfloat16)
        mixed_group = jnp.einsum(
            "mgqk,mkgd->mqgd", soft_b, value_group, preferred_element_type=jnp.float32
        )
        mixed_group = mixed_group.reshape(number_of_realizations, row_count, group_width).astype(
            jnp.bfloat16
        )
        return lax.dynamic_update_slice_in_dim(output, mixed_group, first_col, 2)

    return lax.fori_loop(
        0, model_width // group_width, one_group, jnp.zeros(queries.shape, jnp.bfloat16)
    )


def attention_backward(queries, key_rows, value_rows, allowed, grad_mixed):
    number_of_realizations, row_count, model_width = queries.shape
    key_count = key_rows.shape[1]
    head_size = model_width // HEADS
    group_width = heads_per_group * head_size
    score_scale = 1.0 / math.sqrt(head_size)

    def one_group(group_index, carried):
        grad_query, grad_key, grad_value = carried
        first_col = (group_index * group_width).astype(jnp.int32)
        query_group = split_group(queries, first_col, group_width, head_size)
        key_group = split_group(key_rows, first_col, group_width, head_size)
        value_group = split_group(value_rows, first_col, group_width, head_size)
        upstream_group = split_group(grad_mixed, first_col, group_width, head_size)
        soft = window_probs(query_group, key_group, allowed)
        soft_b = soft.astype(jnp.bfloat16)
        d_soft = jnp.einsum(
            "mqgd,mkgd->mgqk", upstream_group, value_group, preferred_element_type=jnp.float32
        )
        inner_sum = jnp.sum(soft * d_soft, axis=-1, keepdims=True)
        d_score = (soft * (d_soft - inner_sum) * score_scale).astype(jnp.bfloat16)
        query_part = jnp.einsum(
            "mgqk,mkgd->mqgd", d_score, key_group, preferred_element_type=jnp.float32
        )
        key_part = jnp.einsum(
            "mgqk,mqgd->mkgd", d_score, query_group, preferred_element_type=jnp.float32
        )
        value_part = jnp.einsum(
            "mgqk,mqgd->mkgd", soft_b, upstream_group, preferred_element_type=jnp.float32
        )
        grad_query = lax.dynamic_update_slice_in_dim(
            grad_query,
            query_part.reshape(number_of_realizations, row_count, group_width).astype(jnp.bfloat16),
            first_col,
            2,
        )
        grad_key = lax.dynamic_update_slice_in_dim(
            grad_key,
            key_part.reshape(number_of_realizations, key_count, group_width).astype(jnp.bfloat16),
            first_col,
            2,
        )
        grad_value = lax.dynamic_update_slice_in_dim(
            grad_value,
            value_part.reshape(number_of_realizations, key_count, group_width).astype(jnp.bfloat16),
            first_col,
            2,
        )
        return (grad_query, grad_key, grad_value)

    initial = (
        jnp.zeros(queries.shape, jnp.bfloat16),
        jnp.zeros(key_rows.shape, jnp.bfloat16),
        jnp.zeros(value_rows.shape, jnp.bfloat16),
    )
    return lax.fori_loop(0, model_width // group_width, one_group, initial)


def probabilistic_accuracy(predicted_states, measured_part, scaling_coefficient):
    number_of_realizations = predicted_states.shape[0]
    fair_factor = 1.0 - (1.0 - FAIR_ALPHA) / number_of_realizations
    gap_from_measured = predicted_states - measured_part[None]
    smooth_observed = jnp.sqrt(gap_from_measured * gap_from_measured + SMOOTH_WIDTH * SMOOTH_WIDTH)
    between_realization_gap = predicted_states[:, None] - predicted_states[None, :]
    smooth_pair = jnp.sqrt(
        between_realization_gap * between_realization_gap + SMOOTH_WIDTH * SMOOTH_WIDTH
    )
    off_diagonal = (1.0 - jnp.eye(number_of_realizations, dtype=jnp.float32))[:, :, None, None]
    point_score = jnp.sum(smooth_observed, axis=0) / number_of_realizations - fair_factor / (
        2.0 * number_of_realizations * (number_of_realizations - 1)
    ) * jnp.sum(off_diagonal * smooth_pair, axis=(0, 1))
    total = jnp.sum(scaling_coefficient[:, None] * point_score)
    gradient = scaling_coefficient[None, :, None] * (
        gap_from_measured / smooth_observed / number_of_realizations
        - fair_factor
        / (number_of_realizations * (number_of_realizations - 1.0))
        * jnp.sum(between_realization_gap / smooth_pair, axis=1)
    )
    return (total, gradient)


def project_terms(key_part, value_part, w_key, w_value):
    return (times_transposed(key_part, w_key) + times_transposed(value_part, w_value)).astype(
        jnp.bfloat16
    )


def body(
    latent,
    observed,
    area_weight,
    band_counts,
    gain_attn,
    w_query,
    w_key,
    w_value,
    w_out,
    gain_head,
    w_head,
):
    band_index = lax.axis_index("band")
    band_total = lax.axis_size("band")
    member_total = lax.axis_size("member")
    members, slot_count, model_width = latent.shape
    hops = HOPS
    offsets_list = list(range(-hops, hops + 1))
    slot_iota = jnp.arange(slot_count, dtype=jnp.int32)
    offsets = jnp.cumsum(band_counts) - band_counts

    def band_rows(shift_by):
        other = band_index + shift_by
        inside = (other >= 0) & (other < band_total)
        clipped = jnp.clip(other, 0, band_total - 1)
        return (offsets[clipped] + slot_iota, inside & (slot_iota < band_counts[clipped]))

    own_pos, own_live = band_rows(0)
    key_pos = jnp.concatenate([band_rows(offset)[0] for offset in offsets_list])
    key_live = jnp.concatenate([band_rows(offset)[1] for offset in offsets_list])
    allowed = key_live[None, :] & (jnp.abs(own_pos[:, None] - key_pos[None, :]) <= R)
    latent_f = latent.astype(jnp.float32)
    inverse_one = inverse_rms(latent_f)
    normed = (latent_f * inverse_one * gain_attn).astype(jnp.bfloat16)
    queries = jnp.dot(normed, w_query, preferred_element_type=jnp.float32).astype(jnp.bfloat16)
    own_keys = jnp.dot(normed, w_key, preferred_element_type=jnp.float32).astype(jnp.bfloat16)
    own_values = jnp.dot(normed, w_value, preferred_element_type=jnp.float32).astype(jnp.bfloat16)
    key_parts = []
    value_parts = []
    for offset in offsets_list:
        if offset == 0:
            arrived = (own_keys, own_values)
        else:
            arrived = from_behind((own_keys, own_values), "band", -offset)
        key_parts.append(arrived[0])
        value_parts.append(arrived[1])
    key_rows = jnp.concatenate(key_parts, axis=1)
    value_rows = jnp.concatenate(value_parts, axis=1)
    mixed_out = attention_forward(queries, key_rows, value_rows, allowed)
    hidden = latent_f + jnp.dot(mixed_out, w_out, preferred_element_type=jnp.float32)
    inverse_two = inverse_rms(hidden)
    head_in = (hidden * inverse_two * gain_head).astype(jnp.bfloat16)
    predicted = jnp.dot(head_in, w_head, preferred_element_type=jnp.float32).astype(jnp.bfloat16)
    total_live = jnp.sum(band_counts).astype(jnp.float32) * CH
    point_weight = area_weight * own_live.astype(jnp.float32) / total_live
    grouped = lax.all_to_all(predicted, "member", split_axis=1, concat_axis=0, tiled=True)
    point_share = slot_count // member_total
    first_point = lax.axis_index("member") * point_share
    measured_part = lax.dynamic_slice_in_dim(observed, first_point, point_share, 0).astype(
        jnp.float32
    )
    weight_part = lax.dynamic_slice_in_dim(point_weight, first_point, point_share, 0)
    loss_part, gradient = probabilistic_accuracy(
        grouped.astype(jnp.float32), measured_part, weight_part
    )
    grad_pred = lax.all_to_all(
        gradient.astype(jnp.bfloat16), "member", split_axis=0, concat_axis=1, tiled=True
    )
    ensemble_loss = lax.psum(loss_part, ("member", "band"))
    head_share = lax.psum_scatter(
        lax.dot_general(
            head_in, grad_pred, (((0, 1), (0, 1)), ((), ())), preferred_element_type=jnp.float32
        ).astype(jnp.bfloat16),
        "band",
        scatter_dimension=0,
        tiled=True,
    )
    grad_head = lax.psum(head_share, "member").astype(jnp.float32)
    grad_hidden = norm_backward(hidden, gain_head, inverse_two, times_transposed(grad_pred, w_head))
    grad_mixed = times_transposed(grad_hidden.astype(jnp.bfloat16), w_out).astype(jnp.bfloat16)
    grad_queries, key_terms, value_terms = attention_backward(
        queries, key_rows, value_rows, allowed, grad_mixed
    )
    normed_total = jnp.zeros((members, slot_count, model_width), jnp.float32)
    for piece_index, offset in enumerate(offsets_list):
        key_piece = key_terms[:, piece_index * slot_count : (piece_index + 1) * slot_count]
        value_piece = value_terms[:, piece_index * slot_count : (piece_index + 1) * slot_count]
        local_piece = project_terms(key_piece, value_piece, w_key, w_value)
        if offset == 0:
            normed_piece = local_piece
        else:
            normed_piece = from_behind(local_piece, "band", offset)
        normed_total = normed_total + normed_piece.astype(jnp.float32)
    grad_normed = times_transposed(grad_queries, w_query) + normed_total
    grad_latent = (
        grad_hidden + norm_backward(latent_f, gain_attn, inverse_one, grad_normed)
    ).astype(jnp.bfloat16)
    return (grad_latent, grad_head, ensemble_loss)


def solution(mesh):
    placed = (
        P("member", "band", None),
        P("band", None),
        P("band"),
        P(),
        P(),
        P(),
        P(),
        P(),
        P(),
        P(),
        P(),
    )
    return jax.shard_map(
        body,
        mesh=mesh,
        in_specs=placed,
        out_specs=(P("member", "band", None), P("band", None), P()),
        check_vma=False,
    )
```

profile of v0, /device:TPU:0, one launch (start us, length us, event | category | flops | bytes accessed | tf_op | source)
XLA Modules:
  0.0 623.3 jit_solution(18174707358077237049)
XLA Ops:
  21.4 5.5 collective-permute-start.9
  72.4 9.7 %collective-permute-start.1 = (bf16[1,256,1024]{2,1,0:T(8,128)(2,1)S(1)}, bf16[1,256,1024]{2,1,0:T(8,128)(2,1)S(1)}, u32[]{:S(2)}, u32[]{:S(2)}) collective-permute-start(bf16[1,256,1024]{2,1,0:T(8,128)(2,1)S(1)} %copy-done.24), channel_id=1, source_target_pairs={{0,3},{1,4},{2,5},{3,6},{4,7},{8,11},{9,12},{10,13},{11,14},{12,15... | collective-permute-start | bytes 1572872 | tf_op jit(solution)/shard_map/ppermute | solution.py:23
  106.2 6.7 %copy.31 = bf16[1,2304,1024]{1,2,0:T(8,128)(2,1)} copy(bf16[1,2304,1024]{2,1,0:T(8,128)(2,1)} %constant_dynamic-update-slice_fusion.13) | data formatting | bytes 9437184
  115.6 19.4 %collective-permute-done.5 = bf16[1,256,1024]{2,1,0:T(8,128)(2,1)S(1)} collective-permute-done((bf16[1,256,1024]{2,1,0:T(8,128)(2,1)S(1)}, bf16[1,256,1024]{2,1,0:T(8,128)(2,1)S(1)}, u32[]{:S(2)}, u32[]{:S(2)}) %collective-permute-start.5) | collective-permute-done | bytes 524320 | tf_op jit(solution)/shard_map/ppermute | solution.py:23
  142.1 6.7 %copy.29 = bf16[1,2304,1024]{1,2,0:T(8,128)(2,1)} copy(bf16[1,2304,1024]{2,1,0:T(8,128)(2,1)} %constant_dynamic-update-slice_fusion.4) | data formatting | bytes 9437184
  148.9 39.2 %while.32 = (s32[]{:T(128)}, bf16[1,256,1024]{1,2,0:T(8,128)(2,1)S(1)}, bf16[1,2304,1024]{1,2,0:T(8,128)(2,1)}, bf16[1,256,1024]{1,2,0:T(8,128)(2,1)}, bf16[1,23...) while((s32[]{:T(128)}, ...), condition=%wide.region_4.5_spmd.clone, body=%wide.region_2.4_spmd.clone.sunk | while | flops 622918656 | bytes 28529072 | solution.py:79
  196.9 6.0 all-to-all-start
  203.4 5.3 all-to-all-done
  218.3 40.0 %psum.15 = f32[]{:T(128)} all-reduce(f32[]{:T(128)} %multiply_reduce_fusion.2), channel_id=1, replica_groups=mesh['member'=4,'band'=8] {'member','band'}, use_global_device_ids=true, to_apply=%region_19.20 | all-reduce | flops 1 | bytes 8 | tf_op jit(solution)/shard_map/psum | solution.py:240
  271.2 256.9 %while.33 = (s32[]{:T(128)}, bf16[1,256,1024]{1,2,0:T(8,128)(2,1)}, bf16[1,2304,1024]{1,2,0:T(8,128)(2,1)}, bf16[1,2304,1024]{1,2,0:T(8,128)(2,1)}, bf16[1,2304,...) while((s32[]{:T(128)}, bf16[1,256,1024]{1,2,0:T(8,128)(2,1)}, ...), condition=%wide.region_12.13_spmd.clone, body=%wide.region_9.12_spmd.clone.sunk | while | flops 1581979136 | bytes 88961552 | solution.py:139
  277.7 5.0 fusion.220
  282.7 5.6 fusion.222
  288.3 18.9 %fusion.223 = bf16[4,64,256]{2,1,0:T(8,128)(2,1)} fusion(bf16[2304,4,64]{0,2,1:T(8,128)(2,1)S(1)} %bitcast.269, f32[4,256,2304]{2,1,0:T(8,128)} %fusion.220, f32[4,256,2304]{2,1,0:T(8,128)} %get-tuple-element.596, f32[4,256]{1,0:T(4,128)} %get-tuple-element.597, pred[256,2304]{1,0:T(8,128)(4,1)} %copy-done.6), kind=kOutput, calls=%fused_computation.30.clone.1 | convolution fusion | flops 328011008 | bytes 20779008 | tf_op jit(solution)/shard_map/while/body/eval_jaxpr/mgqk,mkgd->mqgd/dot_general | solution.py:105
  307.3 19.5 %fusion.225 = bf16[4,64,2304]{2,1,0:T(8,128)(2,1)S(1)} fusion(bf16[256,4,64]{0,2,1:T(8,128)(2,1)S(1)} %bitcast.275, f32[4,256,2304]{2,1,0:T(8,128)} %fusion.220, f32[4,256,2304]{2,1,0:T(8,128)} %get-tuple-element.596, f32[4,256]{1,0:T(4,128)} %get-tuple-element.597, pred[256,2304]{1,0:T(8,128)(4,1)} %copy-done.6), kind=kOutput, calls=%fused_computation.27.clone.1 | convolution fusion | flops 328535296 | bytes 20779008 | tf_op jit(solution)/shard_map/while/body/eval_jaxpr/mgqk,mqgd->mkgd/dot_general | solution.py:108
  326.8 6.4 %fusion.224 = bf16[4,64,2304]{2,1,0:T(8,128)(2,1)S(1)} fusion(bf16[256,4,64]{0,2,1:T(8,128)(2,1)S(1)} %bitcast.271, f32[4,256,2304]{2,1,0:T(8,128)} %get-tuple-element.596, f32[4,256]{1,0:T(4,128)} %get-tuple-element.597, pred[256,2304]{1,0:T(8,128)(4,1)} %copy-done.6), kind=kOutput, calls=%fused_computation.26.clone.1 | convolution fusion | flops 312016896 | bytes 11341824 | tf_op jit(solution)/shard_map/while/body/eval_jaxpr/mgqk,mqgd->mkgd/dot_general | solution.py:111
  346.8 5.6 fusion.222
  352.4 18.9 %fusion.223 = bf16[4,64,256]{2,1,0:T(8,128)(2,1)} fusion(bf16[2304,4,64]{0,2,1:T(8,128)(2,1)S(1)} %bitcast.269, f32[4,256,2304]{2,1,0:T(8,128)} %fusion.220, f32[4,256,2304]{2,1,0:T(8,128)} %get-tuple-element.596, f32[4,256]{1,0:T(4,128)} %get-tuple-element.597, pred[256,2304]{1,0:T(8,128)(4,1)} %copy-done.6), kind=kOutput, calls=%fused_computation.30.clone.1 | convolution fusion | flops 328011008 | bytes 20779008 | tf_op jit(solution)/shard_map/while/body/eval_jaxpr/mgqk,mkgd->mqgd/dot_general | solution.py:105
  371.4 19.5 %fusion.225 = bf16[4,64,2304]{2,1,0:T(8,128)(2,1)S(1)} fusion(bf16[256,4,64]{0,2,1:T(8,128)(2,1)S(1)} %bitcast.275, f32[4,256,2304]{2,1,0:T(8,128)} %fusion.220, f32[4,256,2304]{2,1,0:T(8,128)} %get-tuple-element.596, f32[4,256]{1,0:T(4,128)} %get-tuple-element.597, pred[256,2304]{1,0:T(8,128)(4,1)} %copy-done.6), kind=kOutput, calls=%fused_computation.27.clone.1 | convolution fusion | flops 328535296 | bytes 20779008 | tf_op jit(solution)/shard_map/while/body/eval_jaxpr/mgqk,mqgd->mkgd/dot_general | solution.py:108
  390.9 6.4 %fusion.224 = bf16[4,64,2304]{2,1,0:T(8,128)(2,1)S(1)} fusion(bf16[256,4,64]{0,2,1:T(8,128)(2,1)S(1)} %bitcast.271, f32[4,256,2304]{2,1,0:T(8,128)} %get-tuple-element.596, f32[4,256]{1,0:T(4,128)} %get-tuple-element.597, pred[256,2304]{1,0:T(8,128)(4,1)} %copy-done.6), kind=kOutput, calls=%fused_computation.26.clone.1 | convolution fusion | flops 312016896 | bytes 11341824 | tf_op jit(solution)/shard_map/while/body/eval_jaxpr/mgqk,mqgd->mkgd/dot_general | solution.py:111
  405.8 5.0 fusion.220
  410.9 5.6 fusion.222
  416.5 18.9 %fusion.223 = bf16[4,64,256]{2,1,0:T(8,128)(2,1)} fusion(bf16[2304,4,64]{0,2,1:T(8,128)(2,1)S(1)} %bitcast.269, f32[4,256,2304]{2,1,0:T(8,128)} %fusion.220, f32[4,256,2304]{2,1,0:T(8,128)} %get-tuple-element.596, f32[4,256]{1,0:T(4,128)} %get-tuple-element.597, pred[256,2304]{1,0:T(8,128)(4,1)} %copy-done.6), kind=kOutput, calls=%fused_computation.30.clone.1 | convolution fusion | flops 328011008 | bytes 20779008 | tf_op jit(solution)/shard_map/while/body/eval_jaxpr/mgqk,mkgd->mqgd/dot_general | solution.py:105
  435.4 19.5 %fusion.225 = bf16[4,64,2304]{2,1,0:T(8,128)(2,1)S(1)} fusion(bf16[256,4,64]{0,2,1:T(8,128)(2,1)S(1)} %bitcast.275, f32[4,256,2304]{2,1,0:T(8,128)} %fusion.220, f32[4,256,2304]{2,1,0:T(8,128)} %get-tuple-element.596, f32[4,256]{1,0:T(4,128)} %get-tuple-element.597, pred[256,2304]{1,0:T(8,128)(4,1)} %copy-done.6), kind=kOutput, calls=%fused_computation.27.clone.1 | convolution fusion | flops 328535296 | bytes 20779008 | tf_op jit(solution)/shard_map/while/body/eval_jaxpr/mgqk,mqgd->mkgd/dot_general | solution.py:108
  454.9 6.4 %fusion.224 = bf16[4,64,2304]{2,1,0:T(8,128)(2,1)S(1)} fusion(bf16[256,4,64]{0,2,1:T(8,128)(2,1)S(1)} %bitcast.271, f32[4,256,2304]{2,1,0:T(8,128)} %get-tuple-element.596, f32[4,256]{1,0:T(4,128)} %get-tuple-element.597, pred[256,2304]{1,0:T(8,128)(4,1)} %copy-done.6), kind=kOutput, calls=%fused_computation.26.clone.1 | convolution fusion | flops 312016896 | bytes 11341824 | tf_op jit(solution)/shard_map/while/body/eval_jaxpr/mgqk,mqgd->mkgd/dot_general | solution.py:111
  469.9 5.0 fusion.220
  474.9 5.6 fusion.222
  480.5 18.9 %fusion.223 = bf16[4,64,256]{2,1,0:T(8,128)(2,1)} fusion(bf16[2304,4,64]{0,2,1:T(8,128)(2,1)S(1)} %bitcast.269, f32[4,256,2304]{2,1,0:T(8,128)} %fusion.220, f32[4,256,2304]{2,1,0:T(8,128)} %get-tuple-element.596, f32[4,256]{1,0:T(4,128)} %get-tuple-element.597, pred[256,2304]{1,0:T(8,128)(4,1)} %copy-done.6), kind=kOutput, calls=%fused_computation.30.clone.1 | convolution fusion | flops 328011008 | bytes 20779008 | tf_op jit(solution)/shard_map/while/body/eval_jaxpr/mgqk,mkgd->mqgd/dot_general | solution.py:105
  499.4 19.5 %fusion.225 = bf16[4,64,2304]{2,1,0:T(8,128)(2,1)S(1)} fusion(bf16[256,4,64]{0,2,1:T(8,128)(2,1)S(1)} %bitcast.275, f32[4,256,2304]{2,1,0:T(8,128)} %fusion.220, f32[4,256,2304]{2,1,0:T(8,128)} %get-tuple-element.596, f32[4,256]{1,0:T(4,128)} %get-tuple-element.597, pred[256,2304]{1,0:T(8,128)(4,1)} %copy-done.6), kind=kOutput, calls=%fused_computation.27.clone.1 | convolution fusion | flops 328535296 | bytes 20779008 | tf_op jit(solution)/shard_map/while/body/eval_jaxpr/mgqk,mqgd->mkgd/dot_general | solution.py:108
  519.0 6.4 %fusion.224 = bf16[4,64,2304]{2,1,0:T(8,128)(2,1)S(1)} fusion(bf16[256,4,64]{0,2,1:T(8,128)(2,1)S(1)} %bitcast.271, f32[4,256,2304]{2,1,0:T(8,128)} %get-tuple-element.596, f32[4,256]{1,0:T(4,128)} %get-tuple-element.597, pred[256,2304]{1,0:T(8,128)(4,1)} %copy-done.6), kind=kOutput, calls=%fused_computation.26.clone.1 | convolution fusion | flops 312016896 | bytes 11341824 | tf_op jit(solution)/shard_map/while/body/eval_jaxpr/mgqk,mqgd->mkgd/dot_general | solution.py:111
  570.8 10.8 %collective-permute-start.23 = (bf16[1,256,1024]{2,1,0:T(8,128)(2,1)}, bf16[1,256,1024]{2,1,0:T(8,128)(2,1)}, u32[]{:S(2)}, u32[]{:S(2)}) collective-permute-start(bf16[1,256,1024]{2,1,0:T(8,128)(2,1)} %fusion.52), channel_id=1, source_target_pairs={{0,4},{1,5},{2,6},{3,7},{8,12},{9,13},{10,14},{11,15},{16,20},{17,... | collective-permute-start | bytes 1572872 | tf_op jit(solution)/shard_map/ppermute | solution.py:23
  581.6 5.1 collective-permute-start.22
  591.3 18.5 %psum.14 = bf16[128,128]{1,0:T(8,128)(2,1)S(1)} all-reduce(bf16[128,128]{1,0:T(8,128)(2,1)} %reduce-scatter.2.cloned.1.call-done), channel_id=1, replica_groups=mesh['member'=4,'band'=8] {'member'}, use_global_device_ids=true, to_apply=%region_15.16 | all-reduce | flops 16384 | bytes 65536 | tf_op jit(solution)/shard_map/psum | solution.py:249
  (297 shorter events, 256.0 us)
Async XLA Ops:
  12.5 86.3 %collective-permute-start.15 = (bf16[1,256,1024]{2,1,0:T(8,128)(2,1)}, bf16[1,256,1024]{2,1,0:T(8,128)(2,1)S(1)}, u32[]{:S(2)}, u32[]{:S(2)}) collective-permute-start(bf16[1,256,1024]{2,1,0:T(8,128)(2,1)} %fusion.64), channel_id=1, source_target_pairs={{4,0},{5,1},{6,2},{7,3},{12,8},{13,9},{14,10},{15,11},{20,16},{21,... | collective-permute-start | bytes 1572872 | tf_op jit(solution)/shard_map/ppermute | solution.py:23
  13.8 53.5 %collective-permute-start.11 = (bf16[1,256,1024]{2,1,0:T(8,128)(2,1)}, bf16[1,256,1024]{2,1,0:T(8,128)(2,1)}, u32[]{:S(2)}, u32[]{:S(2)}) collective-permute-start(bf16[1,256,1024]{2,1,0:T(8,128)(2,1)} %fusion.64), channel_id=1, source_target_pairs={{0,1},{1,2},{2,3},{3,4},{4,5},{5,6},{6,7},{8,9},{9,10},{10,11},{11... | collective-permute-start | bytes 1572872 | tf_op jit(solution)/shard_map/ppermute | solution.py:23
  17.0 47.2 %collective-permute-start.10 = (bf16[1,256,1024]{2,1,0:T(8,128)(2,1)}, bf16[1,256,1024]{2,1,0:T(8,128)(2,1)}, u32[]{:S(2)}, u32[]{:S(2)}) collective-permute-start(bf16[1,256,1024]{2,1,0:T(8,128)(2,1)} %fusion.64), channel_id=1, source_target_pairs={{0,2},{1,3},{2,4},{3,5},{4,6},{5,7},{8,10},{9,11},{10,12},{11,13},... | collective-permute-start | bytes 1572872 | tf_op jit(solution)/shard_map/ppermute | solution.py:23
  21.4 39.6 %collective-permute-start.9 = (bf16[1,256,1024]{2,1,0:T(8,128)(2,1)}, bf16[1,256,1024]{2,1,0:T(8,128)(2,1)}, u32[]{:S(2)}, u32[]{:S(2)}) collective-permute-start(bf16[1,256,1024]{2,1,0:T(8,128)(2,1)} %fusion.64), channel_id=1, source_target_pairs={{0,3},{1,4},{2,5},{3,6},{4,7},{8,11},{9,12},{10,13},{11,14},{12,15... | collective-permute-start | bytes 1572872 | tf_op jit(solution)/shard_map/ppermute | solution.py:23
  26.9 30.9 %collective-permute-start.8 = (bf16[1,256,1024]{2,1,0:T(8,128)(2,1)}, bf16[1,256,1024]{2,1,0:T(8,128)(2,1)}, u32[]{:S(2)}, u32[]{:S(2)}) collective-permute-start(bf16[1,256,1024]{2,1,0:T(8,128)(2,1)} %fusion.64), channel_id=1, source_target_pairs={{0,4},{1,5},{2,6},{3,7},{8,12},{9,13},{10,14},{11,15},{16,20},{17,... | collective-permute-start | bytes 1572872 | tf_op jit(solution)/shard_map/ppermute | solution.py:23
  57.8 14.6 %collective-permute-start = (bf16[1,256,1024]{2,1,0:T(8,128)(2,1)}, bf16[1,256,1024]{2,1,0:T(8,128)(2,1)S(1)}, u32[]{:S(2)}, u32[]{:S(2)}) collective-permute-start(bf16[1,256,1024]{2,1,0:T(8,128)(2,1)} %fusion.62), channel_id=1, source_target_pairs={{0,4},{1,5},{2,6},{3,7},{8,12},{9,13},{10,14},{11,15},{16,20},{17,... | collective-permute-start | bytes 1572872 | tf_op jit(solution)/shard_map/ppermute | solution.py:23
  61.0 22.0 %collective-permute-start.12 = (bf16[1,256,1024]{2,1,0:T(8,128)(2,1)}, bf16[1,256,1024]{2,1,0:T(8,128)(2,1)S(1)}, u32[]{:S(2)}, u32[]{:S(2)}) collective-permute-start(bf16[1,256,1024]{2,1,0:T(8,128)(2,1)} %fusion.64), channel_id=1, source_target_pairs={{1,0},{2,1},{3,2},{4,3},{5,4},{6,5},{7,6},{9,8},{10,9},{11,10},{12... | collective-permute-start | bytes 1572872 | tf_op jit(solution)/shard_map/ppermute | solution.py:23
  64.2 25.9 %collective-permute-start.13 = (bf16[1,256,1024]{2,1,0:T(8,128)(2,1)}, bf16[1,256,1024]{2,1,0:T(8,128)(2,1)S(1)}, u32[]{:S(2)}, u32[]{:S(2)}) collective-permute-start(bf16[1,256,1024]{2,1,0:T(8,128)(2,1)} %fusion.64), channel_id=1, source_target_pairs={{2,0},{3,1},{4,2},{5,3},{6,4},{7,5},{10,8},{11,9},{12,10},{13,11},... | collective-permute-start | bytes 1572872 | tf_op jit(solution)/shard_map/ppermute | solution.py:23
  67.3 29.3 %collective-permute-start.14 = (bf16[1,256,1024]{2,1,0:T(8,128)(2,1)}, bf16[1,256,1024]{2,1,0:T(8,128)(2,1)S(1)}, u32[]{:S(2)}, u32[]{:S(2)}) collective-permute-start(bf16[1,256,1024]{2,1,0:T(8,128)(2,1)} %fusion.64), channel_id=1, source_target_pairs={{3,0},{4,1},{5,2},{6,3},{7,4},{11,8},{12,9},{13,10},{14,11},{15,12... | collective-permute-start | bytes 1572872 | tf_op jit(solution)/shard_map/ppermute | solution.py:23
  72.4 28.5 %collective-permute-start.1 = (bf16[1,256,1024]{2,1,0:T(8,128)(2,1)S(1)}, bf16[1,256,1024]{2,1,0:T(8,128)(2,1)S(1)}, u32[]{:S(2)}, u32[]{:S(2)}) collective-permute-start(bf16[1,256,1024]{2,1,0:T(8,128)(2,1)S(1)} %copy-done.24), channel_id=1, source_target_pairs={{0,3},{1,4},{2,5},{3,6},{4,7},{8,11},{9,12},{10,13},{11,14},{12,15... | collective-permute-start | bytes 1572872 | tf_op jit(solution)/shard_map/ppermute | solution.py:23
  83.0 20.1 %collective-permute-start.2 = (bf16[1,256,1024]{2,1,0:T(8,128)(2,1)S(1)}, bf16[1,256,1024]{2,1,0:T(8,128)(2,1)S(1)}, u32[]{:S(2)}, u32[]{:S(2)}) collective-permute-start(bf16[1,256,1024]{2,1,0:T(8,128)(2,1)S(1)} %copy-done.24), channel_id=1, source_target_pairs={{0,2},{1,3},{2,4},{3,5},{4,6},{5,7},{8,10},{9,11},{10,12},{11,13},... | collective-permute-start | bytes 1572872 | tf_op jit(solution)/shard_map/ppermute | solution.py:23
  90.0 15.3 %collective-permute-start.3 = (bf16[1,256,1024]{2,1,0:T(8,128)(2,1)S(1)}, bf16[1,256,1024]{2,1,0:T(8,128)(2,1)S(1)}, u32[]{:S(2)}, u32[]{:S(2)}) collective-permute-start(bf16[1,256,1024]{2,1,0:T(8,128)(2,1)S(1)} %copy-done.24), channel_id=1, source_target_pairs={{0,1},{1,2},{2,3},{3,4},{4,5},{5,6},{6,7},{8,9},{9,10},{10,11},{11... | collective-permute-start | bytes 1572872 | tf_op jit(solution)/shard_map/ppermute | solution.py:23
  96.6 43.6 %collective-permute-start.7 = (bf16[1,256,1024]{2,1,0:T(8,128)(2,1)S(1)}, bf16[1,256,1024]{2,1,0:T(8,128)(2,1)}, u32[]{:S(2)}, u32[]{:S(2)}) collective-permute-start(bf16[1,256,1024]{2,1,0:T(8,128)(2,1)S(1)} %copy-done.24), channel_id=1, source_target_pairs={{4,0},{5,1},{6,2},{7,3},{12,8},{13,9},{14,10},{15,11},{20,16},{21,... | collective-permute-start | bytes 1572872 | tf_op jit(solution)/shard_map/ppermute | solution.py:23
  98.8 14.9 %collective-permute-start.4 = (bf16[1,256,1024]{2,1,0:T(8,128)(2,1)S(1)}, bf16[1,256,1024]{2,1,0:T(8,128)(2,1)}, u32[]{:S(2)}, u32[]{:S(2)}) collective-permute-start(bf16[1,256,1024]{2,1,0:T(8,128)(2,1)S(1)} %copy-done.24), channel_id=1, source_target_pairs={{1,0},{2,1},{3,2},{4,3},{5,4},{6,5},{7,6},{9,8},{10,9},{11,10},{12... | collective-permute-start | bytes 1572872 | tf_op jit(solution)/shard_map/ppermute | solution.py:23
  100.9 34.1 %collective-permute-start.5 = (bf16[1,256,1024]{2,1,0:T(8,128)(2,1)S(1)}, bf16[1,256,1024]{2,1,0:T(8,128)(2,1)S(1)}, u32[]{:S(2)}, u32[]{:S(2)}) collective-permute-start(bf16[1,256,1024]{2,1,0:T(8,128)(2,1)S(1)} %copy-done.24), channel_id=1, source_target_pairs={{2,0},{3,1},{4,2},{5,3},{6,4},{7,5},{10,8},{11,9},{12,10},{13,11},... | collective-permute-start | bytes 1572872 | tf_op jit(solution)/shard_map/ppermute | solution.py:23
  103.0 35.3 %collective-permute-start.6 = (bf16[1,256,1024]{2,1,0:T(8,128)(2,1)S(1)}, bf16[1,256,1024]{2,1,0:T(8,128)(2,1)}, u32[]{:S(2)}, u32[]{:S(2)}) collective-permute-start(bf16[1,256,1024]{2,1,0:T(8,128)(2,1)S(1)} %copy-done.24), channel_id=1, source_target_pairs={{3,0},{4,1},{5,2},{6,3},{7,4},{11,8},{12,9},{13,10},{14,11},{15,12... | collective-permute-start | bytes 1572872 | tf_op jit(solution)/shard_map/ppermute | solution.py:23
  148.9 43.9 %copy-start.21 = (bf16[1024,128]{1,0:T(8,128)(2,1)S(1)}, bf16[1024,128]{1,0:T(8,128)(2,1)}, u32[]{:S(2)}) copy-start(bf16[1024,128]{1,0:T(8,128)(2,1)} %param.25) | copy-start | bytes 786436
  148.9 43.9 %copy-start.25 = (f32[1024]{0:T(1024)S(1)}, f32[1024]{0:T(1024)}, u32[]{:S(2)}) copy-start(f32[1024]{0:T(1024)} %param.24) | copy-start | bytes 12292
  191.6 73.8 %copy-start.3 = (f32[1,256,1024]{2,1,0:T(8,128)}, f32[1,256,1024]{2,1,0:T(8,128)S(1)}, u32[]{:S(2)}) copy-start(f32[1,256,1024]{2,1,0:T(8,128)S(1)} %get-tuple-element.454) | copy-start | bytes 3145732
  196.9 11.9 %all-to-all-start = ((bf16[4,2,4096]{2,1,0:T(2,128)(2,1)}), bf16[4,2,4096]{2,1,0:T(2,128)(2,1)}, u32[]{:S(2)}, u32[]{:S(2)}) async-start(bf16[4,2,4096]{2,1,0:T(2,128)(2,1)} %reshape.515), calls=%async_computation | async-start | bytes 131072 | tf_op jit(solution)/shard_map/all_to_all | solution.py:227
  213.5 44.8 %all-to-all-start.1 = ((bf16[4,64,128]{2,1,0:T(8,128)(2,1)}), bf16[4,64,128]{2,1,0:T(8,128)(2,1)S(1)}, u32[]{:S(2)}, u32[]{:S(2)}) async-start(bf16[4,64,128]{2,1,0:T(8,128)(2,1)} %get-tuple-element.428), calls=%async_computation.1 | async-start | bytes 131072 | tf_op jit(solution)/shard_map/all_to_all | solution.py:237
  216.8 374.5 %reduce-scatter.2.cloned.1.call-start = ((), (), s32[]{:S(2)}) async-start(), calls=%async_computation.3 | async-start | bytes 294912 | tf_op jit(solution)/shard_map/reduce_scatter | solution.py:241
  548.2 21.1 %collective-permute-start.21 = (bf16[1,256,1024]{2,1,0:T(8,128)(2,1)S(1)}, bf16[1,256,1024]{2,1,0:T(8,128)(2,1)S(1)}, u32[]{:S(2)}, u32[]{:S(2)}) collective-permute-start(bf16[1,256,1024]{2,1,0:T(8,128)(2,1)S(1)} %fusion.54), channel_id=1, source_target_pairs={{0,2},{1,3},{2,4},{3,5},{4,6},{5,7},{8,10},{9,11},{10,12},{11,13},... | collective-permute-start | bytes 1572872 | tf_op jit(solution)/shard_map/ppermute | solution.py:23
  554.8 16.0 %collective-permute-start.20 = (bf16[1,256,1024]{2,1,0:T(8,128)(2,1)S(1)}, bf16[1,256,1024]{2,1,0:T(8,128)(2,1)S(1)}, u32[]{:S(2)}, u32[]{:S(2)}) collective-permute-start(bf16[1,256,1024]{2,1,0:T(8,128)(2,1)S(1)} %fusion.55), channel_id=1, source_target_pairs={{0,1},{1,2},{2,3},{3,4},{4,5},{5,6},{6,7},{8,9},{9,10},{10,11},{11... | collective-permute-start | bytes 1572872 | tf_op jit(solution)/shard_map/ppermute | solution.py:23
  557.1 24.5 %collective-permute-start.19 = (bf16[1,256,1024]{2,1,0:T(8,128)(2,1)S(1)}, bf16[1,256,1024]{2,1,0:T(8,128)(2,1)S(1)}, u32[]{:S(2)}, u32[]{:S(2)}) collective-permute-start(bf16[1,256,1024]{2,1,0:T(8,128)(2,1)S(1)} %fusion.58), channel_id=1, source_target_pairs={{1,0},{2,1},{3,2},{4,3},{5,4},{6,5},{7,6},{9,8},{10,9},{11,10},{12... | collective-permute-start | bytes 1572872 | tf_op jit(solution)/shard_map/ppermute | solution.py:23
  560.1 50.4 %collective-permute-start.18 = (bf16[1,256,1024]{2,1,0:T(8,128)(2,1)}, bf16[1,256,1024]{2,1,0:T(8,128)(2,1)}, u32[]{:S(2)}, u32[]{:S(2)}) collective-permute-start(bf16[1,256,1024]{2,1,0:T(8,128)(2,1)} %fusion.59), channel_id=1, source_target_pairs={{2,0},{3,1},{4,2},{5,3},{6,4},{7,5},{10,8},{11,9},{12,10},{13,11},... | collective-permute-start | bytes 1572872 | tf_op jit(solution)/shard_map/ppermute | solution.py:23
  563.1 47.4 %collective-permute-start.17 = (bf16[1,256,1024]{2,1,0:T(8,128)(2,1)}, bf16[1,256,1024]{2,1,0:T(8,128)(2,1)}, u32[]{:S(2)}, u32[]{:S(2)}) collective-permute-start(bf16[1,256,1024]{2,1,0:T(8,128)(2,1)} %fusion.60), channel_id=1, source_target_pairs={{3,0},{4,1},{5,2},{6,3},{7,4},{11,8},{12,9},{13,10},{14,11},{15,12... | collective-permute-start | bytes 1572872 | tf_op jit(solution)/shard_map/ppermute | solution.py:23
  569.4 41.2 %copy-start.10 = (bf16[1,256,1024]{2,1,0:T(8,128)(2,1)S(1)}, bf16[1,256,1024]{2,1,0:T(8,128)(2,1)}, u32[]{:S(2)}) copy-start(bf16[1,256,1024]{2,1,0:T(8,128)(2,1)} %param.15) | copy-start | bytes 1572868
  569.4 41.2 %copy-start.32 = (f32[1024]{0:T(1024)S(1)}, f32[1024]{0:T(1024)}, u32[]{:S(2)}) copy-start(f32[1024]{0:T(1024)} %param.19) | copy-start | bytes 12292
  569.4 41.1 %collective-permute-start.16 = (bf16[1,256,1024]{2,1,0:T(8,128)(2,1)}, bf16[1,256,1024]{2,1,0:T(8,128)(2,1)}, u32[]{:S(2)}, u32[]{:S(2)}) collective-permute-start(bf16[1,256,1024]{2,1,0:T(8,128)(2,1)} %fusion.61), channel_id=1, source_target_pairs={{4,0},{5,1},{6,2},{7,3},{12,8},{13,9},{14,10},{15,11},{20,16},{21,... | collective-permute-start | bytes 1572872 | tf_op jit(solution)/shard_map/ppermute | solution.py:23
  570.8 39.7 %collective-permute-start.23 = (bf16[1,256,1024]{2,1,0:T(8,128)(2,1)}, bf16[1,256,1024]{2,1,0:T(8,128)(2,1)}, u32[]{:S(2)}, u32[]{:S(2)}) collective-permute-start(bf16[1,256,1024]{2,1,0:T(8,128)(2,1)} %fusion.52), channel_id=1, source_target_pairs={{0,4},{1,5},{2,6},{3,7},{8,12},{9,13},{10,14},{11,15},{16,20},{17,... | collective-permute-start | bytes 1572872 | tf_op jit(solution)/shard_map/ppermute | solution.py:23
  581.6 28.9 %collective-permute-start.22 = (bf16[1,256,1024]{2,1,0:T(8,128)(2,1)}, bf16[1,256,1024]{2,1,0:T(8,128)(2,1)}, u32[]{:S(2)}, u32[]{:S(2)}) collective-permute-start(bf16[1,256,1024]{2,1,0:T(8,128)(2,1)} %fusion.53), channel_id=1, source_target_pairs={{0,3},{1,4},{2,5},{3,6},{4,7},{8,11},{9,12},{10,13},{11,14},{12,15... | collective-permute-start | bytes 1572872 | tf_op jit(solution)/shard_map/ppermute | solution.py:23
  (40 other events, 466.5 us)
Sparse Core Ops, SparseCore 0:
  546.0 34.4 reduce-scatter.1
where the time goes:
time: 632 us; the launch traced here: 623 us
  matrix products  302 us (48%)
  local copies, waits for them, and re-layouts  93.6 us (15%)
  starting transfers between devices  79.4 us (13%)
  blocking collectives  58.5 us (9%)
  other arithmetic  39.5 us (6%)
  waiting for transfers between devices  33 us (5%)
  between operations  15.7 us (2%)
    dot_general x4, matrix products, one_group(): jnp.einsum('mgqk,mqgd->mkgd', d_score, query_group, preferred_element_typ...  78.1 us
    dot_general x4, matrix products, one_group(): jnp.einsum('mgqk,mkgd->mqgd', d_score, key_group, preferred_element_type=...  75.7 us
    ppermute x24, starting transfers between devices, from_behind(): lax.ppermute(value, axis, [(source, source + steps) for source in range(l...  70.1 us
    dot_general x21, matrix products, times_transposed(): lax.dot_general(left_side, scaling_coefficient, (((left_side.ndim - 1,),...  44.2 us
    unnamed x104, local copies, waits for them, and re-layouts  43.2 us
    psum x1, blocking collectives, body(): ensemble_loss = lax.psum(loss_part, ('member', 'band'))  40 us
    dot_general x8, matrix products, window_probs(): jnp.einsum('mqgd,mkgd->mgqk', query_group, key_group, preferred_element_t...  33.5 us
    dynamic_slice x28, local copies, waits for them, and re-layouts, split_group(): part_cols = lax.dynamic_slice_in_dim(array_in, first_col, group_width, 2)  30.3 us
  transfers between devices with their start and end apart: 27, of which 5 were waited for; matrix products, arithmetic and copies ran while one was open for 12% of the time, Pallas kernels for 0%

commit v1 on v0

v1 whole, which is shorter than its diff:
```python
import functools
import math

import jax
import jax.numpy as jnp
from jax import lax
from jax.experimental import pallas as pl
from jax.experimental.pallas import tpu as pltpu
from jax.sharding import PartitionSpec as P

HEADS = 16
CH = 128
R = 512
HOPS = 4


NORM_EPS = 1e-06
SMOOTH_WIDTH = 0.25
FAIR_ALPHA = 0.95
LANES = 128
MASKED = -1e30
VMEM_BYTES = 56 * 1024 * 1024


def inverse_rms(values):
    return lax.rsqrt(jnp.mean(values * values, axis=-1, keepdims=True) + NORM_EPS)


def norm_backward(values, gain_vec, inverse, upstream):
    scaled = upstream * gain_vec
    return inverse * scaled - values * inverse**3 * jnp.mean(
        values * scaled, axis=-1, keepdims=True
    )


def times_transposed(left_side, scaling_coefficient):
    return lax.dot_general(
        left_side,
        scaling_coefficient,
        (((left_side.ndim - 1,), (1,)), ((), ())),
        preferred_element_type=jnp.float32,
    )


def dot_last(left_side, right_side):
    return lax.dot_general(
        left_side, right_side, (((1,), (1,)), ((), ())), preferred_element_type=jnp.float32
    )


def dot_first(left_side, right_side):
    return lax.dot_general(
        left_side, right_side, (((0,), (0,)), ((), ())), preferred_element_type=jnp.float32
    )


def head_masks(shape, dimension, heads, head_size):
    lane = lax.broadcasted_iota(jnp.int32, shape, dimension)
    return [(lane >= h * head_size) & (lane < (h + 1) * head_size) for h in range(heads)]


def masked_heads(block, masks, factor):
    wide = block.astype(jnp.float32) * factor
    return [jnp.where(mask, wide, 0.0).astype(jnp.bfloat16) for mask in masks]


def forward_kernel(
    head_size, tile, reach_ref, q_ref, k_ref, v_ref, bias_ref, out_ref, lse_ref, exp_ref
):
    heads = LANES // head_size
    rows = q_ref.shape[0]
    scale = 1.0 / math.sqrt(head_size)
    masks = head_masks(q_ref.shape, 1, heads, head_size)
    query_heads = masked_heads(q_ref[...], masks, scale)

    def score_step(block, totals):
        at = pl.ds(pl.multiple_of(block * tile, tile), tile)
        keys = k_ref[at, :]
        bias = bias_ref[at, :]
        new = []
        for h in range(heads):
            weight = jnp.exp(dot_last(keys, query_heads[h]) + bias)
            exp_ref[h, at, :] = weight
            new.append(totals[h] + jnp.sum(weight.reshape(tile // 8, 8, rows), axis=0))
        return tuple(new)

    zero = tuple(jnp.zeros((8, rows), jnp.float32) for _ in range(heads))
    partial = lax.fori_loop(reach_ref[0], reach_ref[1], score_step, zero)
    totals = [jnp.sum(part, axis=0, keepdims=True) for part in partial]
    shrink = [jnp.where(total > 1e30, 0.0625, 1.0) for total in totals]
    inverse = [1.0 / (total * small) for total, small in zip(totals, shrink)]

    def value_step(block, mixed):
        at = pl.ds(pl.multiple_of(block * tile, tile), tile)
        values = v_ref[at, :]
        return tuple(
            mixed[h] + dot_first(values, (exp_ref[h, at, :] * inverse[h]).astype(jnp.bfloat16))
            for h in range(heads)
        )

    zero = tuple(jnp.zeros((LANES, rows), jnp.float32) for _ in range(heads))
    mixed = lax.fori_loop(reach_ref[0], reach_ref[1], value_step, zero)
    columns = jnp.concatenate(
        [mixed[h][h * head_size : (h + 1) * head_size] * shrink[h] for h in range(heads)], axis=0
    )
    out_ref[...] = columns.T
    for h in range(heads):
        lse_ref[0, h : h + 1, :] = jnp.log(totals[h])


def backward_kernel(
    head_size,
    tile,
    reach_ref,
    q_ref,
    k_ref,
    v_ref,
    up_ref,
    mixed_ref,
    lse_ref,
    bias_ref,
    dq_ref,
    dk_ref,
    dv_ref,
):
    heads = LANES // head_size
    rows = q_ref.shape[0]
    scale = 1.0 / math.sqrt(head_size)
    masks = head_masks(q_ref.shape, 1, heads, head_size)
    query_heads = masked_heads(q_ref[...], masks, scale)
    up_heads = masked_heads(up_ref[...], masks, 1.0)
    product = (up_ref[...].astype(jnp.float32) * mixed_ref[...]).T
    inner = [
        jnp.sum(product[h * head_size : (h + 1) * head_size], axis=0, keepdims=True)
        for h in range(heads)
    ]
    lse = [lse_ref[0, h : h + 1, :] for h in range(heads)]

    def clear(block, carry):
        at = pl.ds(pl.multiple_of(block * tile, tile), tile)
        dk_ref[at, :] = jnp.zeros((tile, LANES), jnp.bfloat16)
        dv_ref[at, :] = jnp.zeros((tile, LANES), jnp.bfloat16)
        return carry

    lax.fori_loop(0, reach_ref[0], clear, 0)
    lax.fori_loop(reach_ref[1], k_ref.shape[0] // tile, clear, 0)

    def step(block, grads):
        at = pl.ds(pl.multiple_of(block * tile, tile), tile)
        keys = k_ref[at, :]
        values = v_ref[at, :]
        bias = bias_ref[at, :]
        key_sum = jnp.zeros((tile, LANES), jnp.float32)
        value_sum = jnp.zeros((tile, LANES), jnp.float32)
        new = []
        for h in range(heads):
            soft = jnp.exp(dot_last(keys, query_heads[h]) + (bias - lse[h]))
            d_soft = dot_last(values, up_heads[h])
            d_score = (soft * (d_soft - inner[h])).astype(jnp.bfloat16)
            key_sum += jnp.dot(d_score, query_heads[h], preferred_element_type=jnp.float32)
            value_sum += jnp.dot(
                soft.astype(jnp.bfloat16), up_heads[h], preferred_element_type=jnp.float32
            )
            new.append(grads[h] + dot_first(keys, d_score))
        dk_ref[at, :] = key_sum.astype(jnp.bfloat16)
        dv_ref[at, :] = value_sum.astype(jnp.bfloat16)
        return tuple(new)

    zero = tuple(jnp.zeros((LANES, rows), jnp.float32) for _ in range(heads))
    grads = lax.fori_loop(reach_ref[0], reach_ref[1], step, zero)
    columns = jnp.concatenate(
        [grads[h][h * head_size : (h + 1) * head_size] for h in range(heads)], axis=0
    )
    dq_ref[...] = (columns * scale).T.astype(jnp.bfloat16)


def attention_forward(queries, key_rows, value_rows, bias, reach):
    rows, model_width = queries.shape
    slots = key_rows.shape[0]
    head_size = model_width // HEADS
    heads = LANES // head_size
    steps = model_width // LANES
    return pl.pallas_call(
        functools.partial(forward_kernel, head_size, rows),
        grid=(steps,),
        in_specs=[
            pl.BlockSpec(memory_space=pltpu.SMEM),
            pl.BlockSpec((rows, LANES), lambda i: (0, i)),
            pl.BlockSpec((slots, LANES), lambda i: (0, i)),
            pl.BlockSpec((slots, LANES), lambda i: (0, i)),
            pl.BlockSpec((slots, rows), lambda i: (0, 0)),
        ],
        out_specs=[
            pl.BlockSpec((rows, LANES), lambda i: (0, i)),
            pl.BlockSpec((1, heads, rows), lambda i: (i, 0, 0)),
        ],
        out_shape=[
            jax.ShapeDtypeStruct((rows, model_width), jnp.float32),
            jax.ShapeDtypeStruct((steps, heads, rows), jnp.float32),
        ],
        scratch_shapes=[pltpu.VMEM((heads, slots, rows), jnp.float32)],
        compiler_params=pltpu.CompilerParams(vmem_limit_bytes=VMEM_BYTES),
        name="attention_forward",
    )(reach, queries, key_rows, value_rows, bias)


def attention_backward(queries, key_rows, value_rows, upstream, mixed, lse, bias, reach):
    rows, model_width = queries.shape
    slots = key_rows.shape[0]
    head_size = model_width // HEADS
    heads = LANES // head_size
    row_spec = pl.BlockSpec((rows, LANES), lambda i: (0, i))
    slot_spec = pl.BlockSpec((slots, LANES), lambda i: (0, i))
    return pl.pallas_call(
        functools.partial(backward_kernel, head_size, rows),
        grid=(model_width // LANES,),
        in_specs=[
            pl.BlockSpec(memory_space=pltpu.SMEM),
            row_spec,
            slot_spec,
            slot_spec,
            row_spec,
            row_spec,
            pl.BlockSpec((1, heads, rows), lambda i: (i, 0, 0)),
            pl.BlockSpec((slots, rows), lambda i: (0, 0)),
        ],
        out_specs=[row_spec, slot_spec, slot_spec],
        out_shape=[
            jax.ShapeDtypeStruct((rows, model_width), jnp.bfloat16),
            jax.ShapeDtypeStruct((slots, model_width), jnp.bfloat16),
            jax.ShapeDtypeStruct((slots, model_width), jnp.bfloat16),
        ],
        compiler_params=pltpu.CompilerParams(vmem_limit_bytes=VMEM_BYTES),
        name="attention_backward",
    )(reach, queries, key_rows, value_rows, upstream, mixed, lse, bias)


def own_accuracy(own, everyone, member, measured, weight):
    members = everyone.shape[0]
    fair = 1.0 - (1.0 - FAIR_ALPHA) / members
    gap = own - measured
    smooth = jnp.sqrt(gap * gap + SMOOTH_WIDTH * SMOOTH_WIDTH)
    pair_sum = jnp.zeros_like(gap)
    slope_sum = jnp.zeros_like(gap)
    for other in range(members):
        pair_gap = own - everyone[other]
        pair = jnp.sqrt(pair_gap * pair_gap + SMOOTH_WIDTH * SMOOTH_WIDTH)
        pair_sum += jnp.where(member == other, 0.0, pair)
        slope_sum += pair_gap / pair
    score = smooth / members - fair / (2.0 * members * (members - 1)) * pair_sum
    gradient = weight * (gap / smooth / members - fair / (members * (members - 1.0)) * slope_sum)
    return jnp.sum(weight * score), gradient


def body(
    latent,
    observed,
    area_weight,
    band_counts,
    gain_attn,
    w_query,
    w_key,
    w_value,
    w_out,
    gain_head,
    w_head,
):
    band = lax.axis_index("band")
    bands = lax.axis_size("band")
    member = lax.axis_index("member")
    _, slots, model_width = latent.shape
    channels = w_head.shape[1]
    window = min(bands, 2 * HOPS + 1)
    first_band = jnp.clip(band - HOPS, 0, bands - window)

    latent_f = latent[0].astype(jnp.float32)
    inverse_one = inverse_rms(latent_f)
    normed = (latent_f * inverse_one * gain_attn).astype(jnp.bfloat16)
    gathered = lax.all_gather(normed, "band", axis=0, tiled=True)
    normed_rows = lax.dynamic_slice_in_dim(gathered, first_band * slots, window * slots, 0)
    queries = jnp.dot(normed, w_query, preferred_element_type=jnp.float32).astype(jnp.bfloat16)

    slot_iota = jnp.arange(slots, dtype=jnp.int32)
    offsets = jnp.cumsum(band_counts) - band_counts
    own_first = offsets[band]
    own_pos = own_first + slot_iota
    own_live = slot_iota < band_counts[band]
    near = first_band + jnp.arange(window, dtype=jnp.int32)
    near_first = lax.dynamic_slice_in_dim(offsets, first_band, window, 0)
    near_count = lax.dynamic_slice_in_dim(band_counts, first_band, window, 0)
    within = jnp.abs(near - band) <= HOPS
    key_pos = near_first[:, None] + slot_iota[None, :]
    key_live = (slot_iota[None, :] < near_count[:, None]) & within[:, None]
    key_pos = key_pos.reshape(-1)
    allowed = key_live.reshape(-1)[:, None] & (jnp.abs(key_pos[:, None] - own_pos[None, :]) <= R)
    bias = jnp.where(allowed, 0.0, MASKED).astype(jnp.float32)
    reached = (
        within
        & (near_first <= own_first + (slots - 1) + R)
        & (near_first + near_count - 1 >= own_first - R)
    )
    index = jnp.arange(window, dtype=jnp.int32)
    reach = jnp.stack(
        [
            jnp.min(jnp.where(reached, index, window)),
            jnp.max(jnp.where(reached, index + 1, 0)),
        ]
    ).astype(jnp.int32)

    key_rows = jnp.dot(normed_rows, w_key, preferred_element_type=jnp.float32).astype(jnp.bfloat16)
    value_rows = jnp.dot(normed_rows, w_value, preferred_element_type=jnp.float32).astype(
        jnp.bfloat16
    )
    mixed, lse = attention_forward(queries, key_rows, value_rows, bias, reach)
    hidden = latent_f + jnp.dot(
        mixed.astype(jnp.bfloat16), w_out, preferred_element_type=jnp.float32
    )
    inverse_two = inverse_rms(hidden)
    head_in = (hidden * inverse_two * gain_head).astype(jnp.bfloat16)
    predicted = jnp.dot(head_in, w_head, preferred_element_type=jnp.float32).astype(jnp.bfloat16)
    everyone = lax.all_gather(predicted, "member", axis=0, tiled=False)
    total_live = jnp.sum(band_counts).astype(jnp.float32) * CH
    point_weight = area_weight * own_live.astype(jnp.float32) / total_live
    loss_part, gradient = own_accuracy(
        predicted.astype(jnp.float32),
        everyone.astype(jnp.float32),
        member,
        observed.astype(jnp.float32),
        point_weight[:, None],
    )
    grad_pred = gradient.astype(jnp.bfloat16)
    grad_hidden = norm_backward(hidden, gain_head, inverse_two, times_transposed(grad_pred, w_head))
    grad_mixed = times_transposed(grad_hidden.astype(jnp.bfloat16), w_out).astype(jnp.bfloat16)

    head_part = dot_first(head_in, grad_pred).reshape(bands, model_width // bands, channels)
    loss_rows = jnp.broadcast_to(loss_part, (bands, 8, channels))
    packed = jnp.concatenate([head_part, loss_rows], axis=1)
    packed = lax.psum_scatter(packed, "band", scatter_dimension=0, tiled=False)
    packed = jnp.sum(lax.all_gather(packed, "member", axis=0, tiled=False), axis=0)
    grad_head = packed[: model_width // bands]
    ensemble_loss = packed[model_width // bands, 0]

    grad_queries, key_terms, value_terms = attention_backward(
        queries, key_rows, value_rows, grad_mixed, mixed, lse, bias, reach
    )
    terms = (times_transposed(key_terms, w_key) + times_transposed(value_terms, w_value)).astype(
        jnp.bfloat16
    )
    if window < bands:
        terms = lax.dynamic_update_slice_in_dim(
            jnp.zeros((bands * slots, model_width), jnp.bfloat16), terms, first_band * slots, 0
        )
    normed_total = lax.psum_scatter(terms, "band", scatter_dimension=0, tiled=True)
    grad_normed = times_transposed(grad_queries, w_query) + normed_total.astype(jnp.float32)
    grad_latent = (
        grad_hidden + norm_backward(latent_f, gain_attn, inverse_one, grad_normed)
    ).astype(jnp.bfloat16)
    return (grad_latent[None], grad_head, ensemble_loss)


def solution(mesh):
    placed = (
        P("member", "band", None),
        P("band", None),
        P("band"),
        P(),
        P(),
        P(),
        P(),
        P(),
        P(),
        P(),
        P(),
    )
    return jax.shard_map(
        body,
        mesh=mesh,
        in_specs=placed,
        out_specs=(P("member", "band", None), P("band", None), P()),
        check_vma=False,
    )
```

time: 632 us -> 249 us (0.39)
  the two profiles are of different devices: /device:TPU:0 before, /device:TPU:3 now
where the time goes in v1:
time: 249 us; the launch traced here: 247 us
  Pallas kernels  83 us (33%)
  waiting for transfers between devices  63.9 us (26%)
  matrix products  42.8 us (17%)
  blocking collectives  23.9 us (10%)
  between operations  15.9 us (6%)
  other arithmetic  13.2 us (5%)
  local copies, waits for them, and re-layouts  3.97 us (2%)
    pallas_call x1, Pallas kernels, attention_backward(): pl.pallas_call(functools.partial(backward_kernel, head_size, rows), grid=...  50 us
    reduce_scatter x1, waiting for transfers between devices, body(): lax.psum_scatter(terms, 'band', scatter_dimension=0, tiled=True)  39.6 us
    pallas_call x1, Pallas kernels, attention_forward(): pl.pallas_call(functools.partial(forward_kernel, head_size, rows), grid=(...  33.1 us
    all_gather x1, waiting for transfers between devices, body(): gathered = lax.all_gather(normed, 'band', axis=0, tiled=True)  24.2 us
    dot_general x5, matrix products, times_transposed(): lax.dot_general(left_side, scaling_coefficient, (((left_side.ndim - 1,),...  21 us
    all_gather x1, blocking collectives, body(): lax.all_gather(packed, 'member', axis=0, tiled=False)  12.1 us
    all_gather x1, blocking collectives, body(): everyone = lax.all_gather(predicted, 'member', axis=0, tiled=False)  11.8 us
    dot_general x1, matrix products, body(): jnp.dot(normed_rows, w_value, preferred_element_type=jnp.float32)  9.46 us
  transfers between devices with their start and end apart: 3, of which 2 were waited for; matrix products, arithmetic and copies ran while one was open for 12% of the time, Pallas kernels for 20%

profile of v1, /device:TPU:3, one launch (start us, length us, event | category | flops | bytes accessed | tf_op | source)
XLA Modules:
  0.0 247.1 jit_solution(8913556150021352227)
XLA Ops:
  7.2 1.4 fusion.3
  8.6 2.0 fusion.5
  10.8 0.7 dynamic_slice.10
  11.6 0.6 fusion.17
  12.9 0.6 dynamic_slice.4
  15.0 0.6 select_reduce_fusion.1
  15.6 1.9 pad_add_fusion.reach_ref
  17.5 0.6 iota_add_fusion
  18.1 0.7 fusion.15
  18.8 3.5 %convolution_convert_fusion.3.q_ref = bf16[256,1024]{1,0:T(8,128)(2,1)} fusion(bf16[256,1024]{1,0:T(8,128)(2,1)} %fusion.5, bf16[1024,1024]{1,0:T(8,128)(2,1)} %param.16), kind=kOutput, calls=%fused_computation.15 | convolution fusion | flops 537133056 | bytes 3145728 | tf_op jit(solution)/shard_map/dot_general | solution.py:281
  22.3 2.7 %fusion.1.bias_ref = f32[2048,256]{1,0:T(8,128)} fusion(s32[256]{0:T(256)S(1)} %iota_add_fusion, s32[2048]{0:T(1024)S(1)} %bitcast.44, pred[2048]{0:T(1024)(128)(4,1)S(1)} %and.35), kind=kLoop, calls=%fused_computation.10 | loop fusion | flops 2621440 | bytes 2108416 | tf_op jit(solution)/shard_map/jit(_where)/select_n | solution.py:296
  25.0 24.2 %all-gather.3.cloned.1.call-done = bf16[2048,1024]{1,0:T(8,128)(2,1)} async-done(((bf16[256,1024]{1,0:T(8,128)(2,1)}), bf16[2048,1024]{1,0:T(8,128)(2,1)}) %all-gather.3.cloned.1.call-update) | async-done | bytes 4194320 | tf_op jit(solution)/shard_map/all_gather | solution.py:279
  49.2 9.5 %convolution_convert_fusion.v_ref = bf16[2048,1024]{1,0:T(8,128)(2,1)} fusion(bf16[2048,1024]{1,0:T(8,128)(2,1)} %all-gather.3.cloned.1.call-done, bf16[1024,1024]{1,0:T(8,128)(2,1)} %param.18), kind=kOutput, calls=%fused_computation.1 | convolution fusion | flops 4297064448 | bytes 10485760 | tf_op jit(solution)/shard_map/dot_general | solution.py:311
  58.7 6.0 %convolution_convert_fusion.1.k_ref = bf16[2048,1024]{1,0:T(8,128)(2,1)} fusion(bf16[2048,1024]{1,0:T(8,128)(2,1)S(1)} %copy-done.11, bf16[1024,1024]{1,0:T(8,128)(2,1)S(1)} %copy-done), kind=kOutput, calls=%fused_computation.2 | convolution fusion | flops 4297064448 | bytes 10485760 | tf_op jit(solution)/shard_map/dot_general | solution.py:310
  64.7 33.1 %attention_forward.1 = (f32[256,1024]{1,0:T(8,128)}, f32[8,2,256]{2,1,0:T(2,128)}) custom-call(s32[2]{0:T(128)} %pad_add_fusion.reach_ref, bf16[256,1024]{1,0:T(8,128)(2,1)} %convolution_convert_fusion.3.q_ref, bf16[2048,1024]{1,0:T(8,128)(2,1)} %convolution_convert_fusion.1.k_ref, bf16[2048,1024]{1,0:T(8,128)(2,1)} %convolution_convert_fusion.v_ref, ...), custom_call_target="tpu_custom_call" | custom-call | tf_op jit(solution)/shard_map/attention_forward/pallas_call | solution.py:183
  97.8 2.1 multiply_reduce_fusion.1
  99.9 0.3 convolution_convert_fusion.4
  100.3 11.8 %all-gather = bf16[1024,128]{1,0:T(8,128)(2,1)S(1)} all-gather(bf16[256,128]{1,0:T(8,128)(2,1)S(1)} %convolution_convert_fusion.4), channel_id=2, replica_groups=mesh['member'=4,'band'=8] {'member'}, dimensions={0}, use_global_device_ids=true | all-gather | bytes 327680 | tf_op jit(solution)/shard_map/all_gather | solution.py:321
  112.2 1.0 multiply_reduce_fusion.2
  113.1 0.4 fusion.16
  113.5 1.3 multiply_reduce_fusion
  114.8 1.5 concatenate.3
  116.6 3.5 %convolution_convert_fusion.2.up_ref = bf16[256,1024]{1,0:T(8,128)(2,1)} fusion(bf16[1024,1024]{1,0:T(8,128)(2,1)} %param.19, f32[256,1024]{1,0:T(8,128)S(1)} %get-tuple-element.26, f32[256,1024]{1,0:T(8,128)} %get-tuple-element.28, f32[256]{0:T(256)S(1)} %broadcast_multiply_fusion.1, f32[256]{0:T(256)S(1)} %get-tuple-element.21, f32[256]{0:T(256)S(1)} %get-tuple-element.22), kind=kOutput, calls=%fused_computation.14 | convolution fusion | flops 538443776 | bytes 4721664 | tf_op jit(solution)/shard_map/dot_general | solution.py:37
  120.1 50.0 %attention_backward.1 = (bf16[256,1024]{1,0:T(8,128)(2,1)}, bf16[2048,1024]{1,0:T(8,128)(2,1)}, bf16[2048,1024]{1,0:T(8,128)(2,1)}) custom-call(s32[2]{0:T(128)} %pad_add_fusion.reach_ref, bf16[256,1024]{1,0:T(8,128)(2,1)} %convolution_convert_fusion.3.q_ref, bf16[2048,1024]{1,0:T(8,128)(2,1)} %convolution_convert_fusion.1.k_ref, ...), custom_call_target="tpu_custom_call" | custom-call | tf_op jit(solution)/shard_map/attention_backward/pallas_call | solution.py:214
  170.1 6.5 %fusion.18 = f32[2048,1024]{1,0:T(8,128)S(1)} fusion(bf16[2048,1024]{1,0:T(8,128)(2,1)} %get-tuple-element.11, bf16[1024,1024]{1,0:T(8,128)(2,1)S(1)} %copy-done), kind=kOutput, calls=%fused_computation.65 | convolution fusion | flops 4294967296 | bytes 14680064 | tf_op jit(solution)/shard_map/dot_general | solution.py:37
  176.6 6.7 %add_convert_fusion = bf16[2048,1024]{1,0:T(8,128)(2,1)} fusion(f32[2048,1024]{1,0:T(8,128)S(1)} %fusion.18, bf16[2048,1024]{1,0:T(8,128)(2,1)S(1)} %copy-done.12, bf16[1024,1024]{1,0:T(8,128)(2,1)S(1)} %copy-done.13), kind=kOutput, calls=%fused_computation | convolution fusion | flops 4299161600 | bytes 18874368 | tf_op jit(solution)/shard_map/dot_general | solution.py:37
  183.3 12.1 %all_gather.15 = f32[4,136,128]{2,1,0:T(8,128)S(1)} all-gather(f32[1,136,128]{2,1,0:T(8,128)} %reduce-scatter.7.cloned.1.call-done), channel_id=1, replica_groups=mesh['member'=4,'band'=8] {'member'}, dimensions={0}, use_global_device_ids=true | all-gather | bytes 348160 | tf_op jit(solution)/shard_map/all_gather | solution.py:339
  195.5 0.5 slice.33
  196.0 0.6 slice.32
  196.6 39.6 %reduce-scatter.5.cloned.1.call-done = bf16[256,1024]{1,0:T(8,128)(2,1)} async-done(((bf16[2048,1024]{1,0:T(8,128)(2,1)}), bf16[256,1024]{1,0:T(8,128)(2,1)}) %reduce-scatter.5.cloned.1.call-update) | async-done | bytes 524304 | tf_op jit(solution)/shard_map/reduce_scatter | solution.py:353
  236.3 3.0 %fusion.10 = (f32[256]{0:T(256)S(1)}, f32[256,1024]{1,0:T(8,128)S(1)}) fusion(bf16[1,256,1024]{2,1,0:T(8,128)(2,1)} %param.11, f32[1024]{0:T(1024)S(1)} %copy-done.8, bf16[256,1024]{1,0:T(8,128)(2,1)} %reduce-scatter.5.cloned.1.call-done, bf16[256,1024]{1,0:T(8,128)(2,1)} %get-tuple-element.10, bf16[1024,1024]{1,0:T(8,128)(2,1)} %param.16), kind=kOutput, calls=%fused_computation.24 | convolution fusion | flops 538443520 | bytes 4723712 | tf_op jit(solution)/shard_map/dot_general | solution.py:37
  239.4 1.3 fusion.11
  (47 shorter events, 0.9 us)
Async XLA Ops:
  7.2 51.5 %copy-start = (bf16[1024,1024]{1,0:T(8,128)(2,1)S(1)}, bf16[1024,1024]{1,0:T(8,128)(2,1)}, u32[]{:S(2)}) copy-start(bf16[1024,1024]{1,0:T(8,128)(2,1)} %param.17) | copy-start | bytes 6291460
  7.2 3.6 %copy-start.9 = (s32[8]{0:T(128)S(1)}, s32[8]{0:T(128)}, u32[]{:S(2)}) copy-start(s32[8]{0:T(128)} %param.14) | copy-start | bytes 100
  7.2 10.9 %copy-start.10 = (f32[256]{0:T(256)S(1)}, f32[256]{0:T(256)}, u32[]{:S(2)}) copy-start(f32[256]{0:T(256)} %param.13) | copy-start | bytes 3076
  7.2 42.0 %all-gather.3.cloned.1.call-start = ((), (), s32[]{:S(2)}) async-start(), calls=%async_computation.2 | async-start | bytes 4718592 | tf_op jit(solution)/shard_map/all_gather | solution.py:279
  10.7 172.7 %reduce-scatter.7.cloned.1.call-start = ((), (), s32[]{:S(2)}) async-start(), calls=%async_computation.4 | async-start | bytes 626688
  49.2 9.5 %copy-start.11 = (bf16[2048,1024]{1,0:T(8,128)(2,1)S(1)}, bf16[2048,1024]{1,0:T(8,128)(2,1)}, u32[]{:S(2)}) copy-start(bf16[2048,1024]{1,0:T(8,128)(2,1)} %all-gather.3.cloned.1.call-done) | copy-start | bytes 12582916
  64.7 33.1 %copy-start.1 = (bf16[1,256,1024]{2,1,0:T(8,128)(2,1)S(1)}, bf16[1,256,1024]{2,1,0:T(8,128)(2,1)}, u32[]{:S(2)}) copy-start(bf16[1,256,1024]{2,1,0:T(8,128)(2,1)} %param.11) | copy-start | bytes 1572868
  64.7 33.1 %copy-start.4 = (bf16[1024,1024]{1,0:T(8,128)(2,1)S(1)}, bf16[1024,1024]{1,0:T(8,128)(2,1)}, u32[]{:S(2)}) copy-start(bf16[1024,1024]{1,0:T(8,128)(2,1)} %param.19) | copy-start | bytes 6291460
  97.8 2.1 copy-start.5
  97.8 2.1 copy-start.7
  99.9 12.2 %copy-start.6 = (bf16[256,128]{1,0:T(8,128)(2,1)S(1)}, bf16[256,128]{1,0:T(8,128)(2,1)}, u32[]{:S(2)}) copy-start(bf16[256,128]{1,0:T(8,128)(2,1)} %param.12) | copy-start | bytes 196612
  116.3 119.9 %reduce-scatter.5.cloned.1.call-start = ((), (), s32[]{:S(2)}) async-start(), calls=%async_computation.3 | async-start | bytes 4718592 | tf_op jit(solution)/shard_map/reduce_scatter | solution.py:353
  170.1 6.5 %copy-start.12 = (bf16[2048,1024]{1,0:T(8,128)(2,1)S(1)}, bf16[2048,1024]{1,0:T(8,128)(2,1)}, u32[]{:S(2)}) copy-start(bf16[2048,1024]{1,0:T(8,128)(2,1)} %get-tuple-element.12) | copy-start | bytes 12582916
  170.1 6.5 %copy-start.13 = (bf16[1024,1024]{1,0:T(8,128)(2,1)S(1)}, bf16[1024,1024]{1,0:T(8,128)(2,1)}, u32[]{:S(2)}) copy-start(bf16[1024,1024]{1,0:T(8,128)(2,1)} %param.18) | copy-start | bytes 6291460
  183.3 53.0 %copy-start.8 = (f32[1024]{0:T(1024)S(1)}, f32[1024]{0:T(1024)}, u32[]{:S(2)}) copy-start(f32[1024]{0:T(1024)} %param.15) | copy-start | bytes 12292
  236.3 3.1 %copy-start.2 = (bf16[1,256,1024]{2,1,0:T(8,128)(2,1)S(1)}, bf16[1,256,1024]{2,1,0:T(8,128)(2,1)}, u32[]{:S(2)}) copy-start(bf16[1,256,1024]{2,1,0:T(8,128)(2,1)} %param.11) | copy-start | bytes 1572868
  236.3 3.1 %copy-start.3 = (f32[256,1024]{1,0:T(8,128)S(1)}, f32[256,1024]{1,0:T(8,128)}, u32[]{:S(2)}) copy-start(f32[256,1024]{1,0:T(8,128)} %get-tuple-element.28) | copy-start | bytes 3145732
Sparse Core Ops, SparseCore 0:
  10.8 38.3 all-gather.2
  116.5 34.2 reduce-scatter.6
  183.4 52.8 reduce-scatter.4

commit v2 on v1

--- a/solution.py
+++ b/solution.py
@@ -235,17 +235,333 @@
     )(reach, queries, key_rows, value_rows, upstream, mixed, lse, bias)
 
 
-def own_accuracy(own, everyone, member, measured, weight):
-    members = everyone.shape[0]
+MESH = pl.DeviceIdType.MESH
+COLUMNS = 256
+
+
+def partner(index, distance):
+    bit = 1
+    flipped = index
+    while bit <= distance:
+        if distance & bit:
+            flipped = flipped + (1 - 2 * ((index // bit) % 2)) * bit
+        bit *= 2
+    return flipped
+
+
+def band_layout():
+    band = lax.axis_index("band")
+    return lax.axis_index("member"), band, band // 2, band % 2
+
+
+def far_first(pairs):
+    return sorted(range(1, pairs), key=lambda d: (-bin(d).count("1"), d))
+
+
+def greet(targets):
+    barrier = pltpu.get_barrier_semaphore()
+    for target in targets:
+        pl.semaphore_signal(barrier, inc=1, device_id=target, device_id_type=MESH)
+    pl.semaphore_wait(barrier, len(targets))
+
+
+def send(source, target_ref, send_sem, recv_sem, target):
+    return pltpu.make_async_remote_copy(
+        src_ref=source,
+        dst_ref=target_ref,
+        send_sem=send_sem,
+        recv_sem=recv_sem,
+        device_id=target,
+        device_id_type=MESH,
+    )
+
+
+def project_into(rows_ref, weight_ref, out_ref):
+    @pl.loop(0, weight_ref.shape[1] // COLUMNS)
+    def _(tile):
+        at = pl.ds(pl.multiple_of(tile * COLUMNS, COLUMNS), COLUMNS)
+        out_ref[:, at] = jnp.dot(
+            rows_ref[...], weight_ref[:, at], preferred_element_type=jnp.float32
+        ).astype(out_ref.dtype)
+
+
+def gather_kernel(
+    bands,
+    window,
+    normed_ref,
+    wq_ref,
+    wk_ref,
+    wv_ref,
+    q_ref,
+    k_ref,
+    v_ref,
+    held,
+    send_sem,
+    recv_sem,
+    pass_send,
+    pass_recv,
+):
+    member, band, pair, core = band_layout()
+    pairs = bands // 2
+    slots = normed_ref.shape[0]
+    sibling = (member, 2 * pair + 1 - core)
+    order = far_first(pairs)
+    targets = {d: (member, 2 * partner(pair, d) + core) for d in order}
+    greet([sibling] + [targets[d] for d in order])
+    copies = {
+        d: send(normed_ref, held.at[band], send_sem.at[d], recv_sem.at[d], targets[d])
+        for d in order
+    }
+    copies[0] = send(normed_ref, held.at[band], send_sem.at[0], recv_sem.at[0], sibling)
+    for d in order + [0]:
+        copies[d].start()
+    first = jnp.clip(band - HOPS, 0, bands - window)
+
+    def project(rows_ref, source):
+        def run():
+            place = pl.ds(pl.multiple_of((source - first) * slots, slots), slots)
+            project_into(rows_ref, wk_ref, k_ref.at[place])
+            project_into(rows_ref, wv_ref, v_ref.at[place])
+
+        if window == bands:
+            run()
+        else:
+            pl.when((source >= first) & (source < first + window))(run)
+
+    project_into(normed_ref, wq_ref, q_ref)
+    project(normed_ref, band)
+    copies[0].wait_recv()
+    project(held.at[2 * pair + 1 - core], 2 * pair + 1 - core)
+    passes = {}
+    near_first = order[::-1]
+    for d in near_first:
+        copies[d].wait_recv()
+        source = 2 * partner(pair, d) + core
+        passes[d] = send(
+            held.at[source], held.at[source], pass_send.at[d], pass_recv.at[d], sibling
+        )
+        passes[d].start()
+        project(held.at[source], source)
+    for d in near_first:
+        passes[d].wait_recv()
+        source = 2 * partner(pair, d) + 1 - core
+        project(held.at[source], source)
+    for d in order + [0]:
+        copies[d].wait_send()
+    for d in order:
+        passes[d].wait_send()
+
+
+def gather_and_project(normed, w_query, w_key, w_value, bands, window):
+    slots, model_width = normed.shape
+    vmem = pl.BlockSpec(memory_space=pltpu.VMEM)
+    pairs = bands // 2
+    return pl.pallas_call(
+        functools.partial(gather_kernel, bands, window),
+        in_specs=[vmem] * 4,
+        out_specs=[vmem] * 3,
+        out_shape=[
+            jax.ShapeDtypeStruct((slots, model_width), jnp.bfloat16),
+            jax.ShapeDtypeStruct((window * slots, model_width), jnp.bfloat16),
+            jax.ShapeDtypeStruct((window * slots, model_width), jnp.bfloat16),
+        ],
+        scratch_shapes=[
+            pltpu.VMEM((bands, slots, model_width), jnp.bfloat16),
+            pltpu.SemaphoreType.DMA((pairs,)),
+            pltpu.SemaphoreType.DMA((pairs,)),
+            pltpu.SemaphoreType.DMA((pairs,)),
+            pltpu.SemaphoreType.DMA((pairs,)),
+        ],
+        compiler_params=pltpu.CompilerParams(
+            collective_id=0, has_side_effects=True, vmem_limit_bytes=VMEM_BYTES
+        ),
+        name="gather_rows",
+    )(normed, w_query, w_key, w_value)
+
+
+def member_targets(members):
+    member = lax.axis_index("member")
+    band = lax.axis_index("band")
+    return [(lax.rem(member + d, members), band) for d in range(1, members)]
+
+
+def exchange_kernel(members, own_ref, all_ref, held, send_sem, recv_sem):
+    targets = member_targets(members)
+    greet(targets)
+    copies = [
+        send(own_ref, held.at[d], send_sem.at[d], recv_sem.at[d], targets[d])
+        for d in range(members - 1)
+    ]
+    for copy in copies:
+        copy.start()
+    for d, copy in enumerate(copies):
+        copy.wait_recv()
+        all_ref[d] = held[d]
+    for copy in copies:
+        copy.wait_send()
+
+
+def exchange_members(own, members):
+    vmem = pl.BlockSpec(memory_space=pltpu.VMEM)
+    return pl.pallas_call(
+        functools.partial(exchange_kernel, members),
+        in_specs=[vmem],
+        out_specs=vmem,
+        out_shape=jax.ShapeDtypeStruct((members - 1,) + own.shape, own.dtype),
+        scratch_shapes=[
+            pltpu.VMEM((members - 1,) + own.shape, own.dtype),
+            pltpu.SemaphoreType.DMA((members - 1,)),
+            pltpu.SemaphoreType.DMA((members - 1,)),
+        ],
+        compiler_params=pltpu.CompilerParams(collective_id=1, has_side_effects=True),
+        name="exchange_members",
+    )(own)
+
+
+def terms_kernel(
+    bands,
+    members,
+    window,
+    dk_ref,
+    dv_ref,
+    wk_ref,
+    wv_ref,
+    head_ref,
+    total_ref,
+    head_out,
+    for_sibling,
+    from_sibling,
+    outgoing,
+    arriving,
+    head_held,
+    sib_send,
+    sib_recv,
+    far_send,
+    far_recv,
+    head_send,
+    head_recv,
+):
+    member, band, pair, core = band_layout()
+    pairs = bands // 2
+    slots = total_ref.shape[0]
+    sibling = (member, 2 * pair + 1 - core)
+    order = far_first(pairs)
+    targets = {d: (member, 2 * partner(pair, d) + core) for d in order}
+    others = member_targets(members)
+    greet([sibling] + [targets[d] for d in order] + others)
+    head_copies = [
+        send(head_ref, head_held.at[member], head_send.at[d], head_recv.at[d], others[d])
+        for d in range(members - 1)
+    ]
+    for copy in head_copies:
+        copy.start()
+    first = jnp.clip(band - HOPS, 0, bands - window)
+
+    def project(target, out_ref):
+        def run():
+            place = pl.ds(pl.multiple_of((target - first) * slots, slots), slots)
+
+            @pl.loop(0, wk_ref.shape[0] // COLUMNS)
+            def _(tile):
+                at = pl.ds(pl.multiple_of(tile * COLUMNS, COLUMNS), COLUMNS)
+                out_ref[:, at] = (
+                    dot_last(dk_ref[place, :], wk_ref[at, :])
+                    + dot_last(dv_ref[place, :], wv_ref[at, :])
+                ).astype(out_ref.dtype)
+
+        if window == bands:
+            run()
+        else:
+            inside = (target >= first) & (target < first + window)
+            pl.when(inside)(run)
+
+            @pl.when(jnp.logical_not(inside))
+            def _():
+                out_ref[...] = jnp.zeros(out_ref.shape, out_ref.dtype)
+
+    near = {}
+    far = {}
+    for d in order + [0]:
+        there = partner(pair, d)
+        project(2 * there + 1 - core, for_sibling.at[d])
+        near[d] = send(
+            for_sibling.at[d], from_sibling.at[d], sib_send.at[d], sib_recv.at[d], sibling
+        )
+        near[d].start()
+        project(2 * there + core, outgoing.at[d])
+        near[d].wait_recv()
+        if d:
+            outgoing[d] = (
+                outgoing[d].astype(jnp.float32) + from_sibling[d].astype(jnp.float32)
+            ).astype(jnp.bfloat16)
+            far[d] = send(
+                outgoing.at[d], arriving.at[d], far_send.at[d], far_recv.at[d], targets[d]
+            )
+            far[d].start()
+        else:
+            total_ref[...] = outgoing[0].astype(jnp.float32) + from_sibling[0].astype(jnp.float32)
+    head_held[member] = head_ref[...]
+    for copy in head_copies:
+        copy.wait_recv()
+    head_sum = head_held[0]
+    for other in range(1, members):
+        head_sum += head_held[other]
+    head_out[...] = head_sum
+    for d in order:
+        far[d].wait_recv()
+        total_ref[...] += arriving[d].astype(jnp.float32)
+    for d in order:
+        far[d].wait_send()
+        near[d].wait_send()
+    near[0].wait_send()
+    for copy in head_copies:
+        copy.wait_send()
+
+
+def project_and_return(key_terms, value_terms, w_key, w_value, head, bands, members, window):
+    slots, model_width = key_terms.shape[0] // window, key_terms.shape[1]
+    vmem = pl.BlockSpec(memory_space=pltpu.VMEM)
+    pairs = bands // 2
+    blocks = pltpu.VMEM((pairs, slots, model_width), jnp.bfloat16)
+    return pl.pallas_call(
+        functools.partial(terms_kernel, bands, members, window),
+        in_specs=[vmem] * 5,
+        out_specs=[vmem] * 2,
+        out_shape=[
+            jax.ShapeDtypeStruct((slots, model_width), jnp.float32),
+            jax.ShapeDtypeStruct(head.shape, jnp.float32),
+        ],
+        scratch_shapes=[
+            blocks,
+            blocks,
+            blocks,
+            blocks,
+            pltpu.VMEM((members,) + head.shape, jnp.float32),
+            pltpu.SemaphoreType.DMA((pairs,)),
+            pltpu.SemaphoreType.DMA((pairs,)),
+            pltpu.SemaphoreType.DMA((pairs,)),
+            pltpu.SemaphoreType.DMA((pairs,)),
+            pltpu.SemaphoreType.DMA((members - 1,)),
+            pltpu.SemaphoreType.DMA((members - 1,)),
+        ],
+        compiler_params=pltpu.CompilerParams(
+            collective_id=2, has_side_effects=True, vmem_limit_bytes=VMEM_BYTES
+        ),
+        name="return_terms",
+    )(key_terms, value_terms, w_key, w_value, head)
+
+
+def own_accuracy(own, others, measured, weight):
+    members = others.shape[0] + 1
     fair = 1.0 - (1.0 - FAIR_ALPHA) / members
     gap = own - measured
     smooth = jnp.sqrt(gap * gap + SMOOTH_WIDTH * SMOOTH_WIDTH)
     pair_sum = jnp.zeros_like(gap)
     slope_sum = jnp.zeros_like(gap)
-    for other in range(members):
-        pair_gap = own - everyone[other]
+    for other in range(members - 1):
+        pair_gap = own - others[other]
         pair = jnp.sqrt(pair_gap * pair_gap + SMOOTH_WIDTH * SMOOTH_WIDTH)
-        pair_sum += jnp.where(member == other, 0.0, pair)
+        pair_sum += pair
         slope_sum += pair_gap / pair
     score = smooth / members - fair / (2.0 * members * (members - 1)) * pair_sum
     gradient = weight * (gap / smooth / members - fair / (members * (members - 1.0)) * slope_sum)
@@ -267,7 +583,7 @@
 ):
     band = lax.axis_index("band")
     bands = lax.axis_size("band")
-    member = lax.axis_index("member")
+    members = lax.axis_size("member")
     _, slots, model_width = latent.shape
     channels = w_head.shape[1]
     window = min(bands, 2 * HOPS + 1)
@@ -276,9 +592,9 @@
     latent_f = latent[0].astype(jnp.float32)
     inverse_one = inverse_rms(latent_f)
     normed = (latent_f * inverse_one * gain_attn).astype(jnp.bfloat16)
-    gathered = lax.all_gather(normed, "band", axis=0, tiled=True)
-    normed_rows = lax.dynamic_slice_in_dim(gathered, first_band * slots, window * slots, 0)
-    queries = jnp.dot(normed, w_query, preferred_element_type=jnp.float32).astype(jnp.bfloat16)
+    queries, key_rows, value_rows = gather_and_project(
+        normed, w_query, w_key, w_value, bands, window
+    )
 
     slot_iota = jnp.arange(slots, dtype=jnp.int32)
     offsets = jnp.cumsum(band_counts) - band_counts
@@ -307,10 +623,6 @@
         ]
     ).astype(jnp.int32)
 
-    key_rows = jnp.dot(normed_rows, w_key, preferred_element_type=jnp.float32).astype(jnp.bfloat16)
-    value_rows = jnp.dot(normed_rows, w_value, preferred_element_type=jnp.float32).astype(
-        jnp.bfloat16
-    )
     mixed, lse = attention_forward(queries, key_rows, value_rows, bias, reach)
     hidden = latent_f + jnp.dot(
         mixed.astype(jnp.bfloat16), w_out, preferred_element_type=jnp.float32
@@ -318,13 +630,12 @@
     inverse_two = inverse_rms(hidden)
     head_in = (hidden * inverse_two * gain_head).astype(jnp.bfloat16)
     predicted = jnp.dot(head_in, w_head, preferred_element_type=jnp.float32).astype(jnp.bfloat16)
-    everyone = lax.all_gather(predicted, "member", axis=0, tiled=False)
+    others = exchange_members(predicted, members)
     total_live = jnp.sum(band_counts).astype(jnp.float32) * CH
     point_weight = area_weight * own_live.astype(jnp.float32) / total_live
     loss_part, gradient = own_accuracy(
         predicted.astype(jnp.float32),
-        everyone.astype(jnp.float32),
-        member,
+        others.astype(jnp.float32),
         observed.astype(jnp.float32),
         point_weight[:, None],
     )
@@ -336,22 +647,15 @@
     loss_rows = jnp.broadcast_to(loss_part, (bands, 8, channels))
     packed = jnp.concatenate([head_part, loss_rows], axis=1)
     packed = lax.psum_scatter(packed, "band", scatter_dimension=0, tiled=False)
-    packed = jnp.sum(lax.all_gather(packed, "member", axis=0, tiled=False), axis=0)
+    grad_queries, key_terms, value_terms = attention_backward(
+        queries, key_rows, value_rows, grad_mixed, mixed, lse, bias, reach
+    )
+    normed_total, packed = project_and_return(
+        key_terms, value_terms, w_key, w_value, packed, bands, members, window
+    )
     grad_head = packed[: model_width // bands]
     ensemble_loss = packed[model_width // bands, 0]
-
-    grad_queries, key_terms, value_terms = attention_backward(
-        queries, key_rows, value_rows, grad_mixed, mixed, lse, bias, reach
-    )
-    terms = (times_transposed(key_terms, w_key) + times_transposed(value_terms, w_value)).astype(
-        jnp.bfloat16
-    )
-    if window < bands:
-        terms = lax.dynamic_update_slice_in_dim(
-            jnp.zeros((bands * slots, model_width), jnp.bfloat16), terms, first_band * slots, 0
-        )
-    normed_total = lax.psum_scatter(terms, "band", scatter_dimension=0, tiled=True)
-    grad_normed = times_transposed(grad_queries, w_query) + normed_total.astype(jnp.float32)
+    grad_normed = times_transposed(grad_queries, w_query) + normed_total
     grad_latent = (
         grad_hidden + norm_backward(latent_f, gain_attn, inverse_one, grad_normed)
     ).astype(jnp.bfloat16)

time: 249 us -> 228 us (0.916)
  Pallas kernels: 83 us -> 174 us
  waiting for transfers between devices: 63.9 us -> 0.04 us
  matrix products: 42.8 us -> 8.69 us
  blocking collectives: 23.9 us -> 0 us
  other arithmetic: 13.2 us -> 18.2 us
  local copies, waits for them, and re-layouts: 3.97 us -> 6.76 us
    pallas_call x0 -> x3, Pallas kernels: none -> 91.1 us  [the longest x1 46.9 us: gather_and_project(): pl.pallas_call(functools.partial(gather_kernel, bands, window), in_specs=...]
    reduce_scatter x1 -> x0, waiting for transfers between devices: 39.6 us -> none  [body(): lax.psum_scatter(terms, 'band', scatter_dimension=0, tiled=True)]
    all_gather x1 -> x0, waiting for transfers between devices: 24.2 us -> none  [body(): gathered = lax.all_gather(normed, 'band', axis=0, tiled=True)]
    all_gather x2 -> x0, blocking collectives: 23.9 us -> none  [the longest x1 12.1 us: body(): lax.all_gather(packed, 'member', axis=0, tiled=False)]
    dot_general x3 -> x0, matrix products: 19 us -> none  [the longest x1 9.46 us: body(): jnp.dot(normed_rows, w_value, preferred_element_type=jnp.float32)]
    dot_general x5 -> x3, matrix products: 21 us -> 5.22 us  [times_transposed(): lax.dot_general(left_side, scaling_coefficient, (((left_side.ndim - 1,),...]
  transfers between devices with their start and end apart: 3 -> 1, of which waited for: 2 -> 0; matrix products, arithmetic and copies ran while one was open for 12% -> 1% of each run, Pallas kernels for 20% -> 22%
where the time goes in v2:
time: 228 us; the launch traced here: 224 us
  Pallas kernels  174 us (76%)
  other arithmetic  18.2 us (8%)
  between operations  16.2 us (7%)
  matrix products  8.69 us (4%)
  local copies, waits for them, and re-layouts  6.76 us (3%)
    pallas_call x1, Pallas kernels, attention_backward(): pl.pallas_call(functools.partial(backward_kernel, head_size, rows), grid=...  50 us
    pallas_call x1, Pallas kernels, gather_and_project(): pl.pallas_call(functools.partial(gather_kernel, bands, window), in_specs=...  46.9 us
    pallas_call x1, Pallas kernels, project_and_return(): pl.pallas_call(functools.partial(terms_kernel, bands, members, window), i...  36.1 us
    pallas_call x1, Pallas kernels, attention_forward(): pl.pallas_call(functools.partial(forward_kernel, head_size, rows), grid=(...  33 us
    pallas_call x1, Pallas kernels, exchange_members(): pl.pallas_call(functools.partial(exchange_kernel, members), in_specs=[vme...  8.12 us
    dot_general x3, matrix products, times_transposed(): lax.dot_general(left_side, scaling_coefficient, (((left_side.ndim - 1,),...  5.22 us
  transfers between devices with their start and end apart: 1, of which 0 were waited for; matrix products, arithmetic and copies ran while one was open for 1% of the time, Pallas kernels for 22%

profile of v2, /device:TPU:3, one launch (start us, length us, event | category | flops | bytes accessed | tf_op | source)
XLA Modules:
  0.0 224.0 jit_solution(393140720171438955)
XLA Ops:
  7.2 1.0 reduce-window.9
  8.2 1.3 fusion.17
  9.5 0.1 add_bitcast_fusion
  9.6 0.6 dynamic_slice.8
  10.1 1.3 dynamic_slice.9
  11.5 0.6 iota_add_fusion
  13.4 0.6 select_reduce_fusion.1
  14.1 1.2 fusion.3
  15.3 0.6 multiply_multiply_fusion
  15.9 0.7 fusion.14
  16.7 2.0 pad_add_fusion.reach_ref
  18.6 2.0 fusion.5.normed_ref
  20.6 2.7 %fusion.1.bias_ref = f32[2048,256]{1,0:T(8,128)} fusion(s32[256]{0:T(256)S(1)} %iota_add_fusion, s32[2048]{0:T(1024)S(1)} %bitcast.60, pred[2048]{0:T(1024)(128)(4,1)S(1)} %and.34), kind=kLoop, calls=%fused_computation.7 | loop fusion | flops 2621440 | bytes 2108416 | tf_op jit(solution)/shard_map/jit(_where)/select_n | solution.py:612
  23.3 46.9 %gather_rows.1 = (bf16[256,1024]{1,0:T(8,128)(2,1)}, bf16[2048,1024]{1,0:T(8,128)(2,1)}, bf16[2048,1024]{1,0:T(8,128)(2,1)}) custom-call(bf16[256,1024]{1,0:T(8,128)(2,1)} %fusion.5.normed_ref, bf16[1024,1024]{1,0:T(8,128)(2,1)} %wq_ref.1, bf16[1024,1024]{1,0:T(8,128)(2,1)} %wk_ref.3, bf16[1024,1024]{1,0:T(8,128)(2,1)} %wv_ref.3), custom_call_target="tpu_custom_call" | custom-call | tf_op jit(solution)/shard_map/gather_rows/pallas_call | solution.py:359
  70.3 33.0 %attention_forward.1 = (f32[256,1024]{1,0:T(8,128)}, f32[8,2,256]{2,1,0:T(2,128)}) custom-call(s32[2]{0:T(128)} %pad_add_fusion.reach_ref, bf16[256,1024]{1,0:T(8,128)(2,1)} %get-tuple-element.13.q_ref, bf16[2048,1024]{1,0:T(8,128)(2,1)} %get-tuple-element.14.k_ref, bf16[2048,1024]{1,0:T(8,128)(2,1)} %get-tuple-element.15.v_ref, f32[2048,256]{1,0:T(8,128)} %fusion.1.bias_ref), custom_call_target="tpu_custom_call" | custom-call | tf_op jit(solution)/shard_map/attention_forward/pallas_call | solution.py:183
  103.3 2.1 multiply_reduce_fusion.1
  105.4 1.0 convolution_convert_fusion.1.own_ref
  106.4 8.1 %exchange_members.1 = bf16[3,256,128]{2,1,0:T(8,128)(2,1)} custom-call(bf16[256,128]{1,0:T(8,128)(2,1)} %convolution_convert_fusion.1.own_ref), custom_call_target="tpu_custom_call" | custom-call | tf_op jit(solution)/shard_map/exchange_members/pallas_call | solution.py:406
  114.5 1.0 convert_element_type.52
  116.1 1.4 fusion.15
  117.5 1.8 multiply_reduce_fusion.2
  119.3 0.6 copy-done.8
  119.9 0.4 fusion.16
  120.3 1.5 concatenate.3
  121.8 1.2 multiply_reduce_fusion
  123.1 1.6 convolution_convert_fusion.up_ref
  124.7 50.0 %attention_backward.1 = (bf16[256,1024]{1,0:T(8,128)(2,1)}, bf16[2048,1024]{1,0:T(8,128)(2,1)}, bf16[2048,1024]{1,0:T(8,128)(2,1)}) custom-call(s32[2]{0:T(128)} %pad_add_fusion.reach_ref, bf16[256,1024]{1,0:T(8,128)(2,1)} %get-tuple-element.13.q_ref, bf16[2048,1024]{1,0:T(8,128)(2,1)} %get-tuple-element.14.k_ref, ...), custom_call_target="tpu_custom_call" | custom-call | tf_op jit(solution)/shard_map/attention_backward/pallas_call | solution.py:214
  174.8 36.1 %return_terms.1 = (f32[256,1024]{1,0:T(8,128)}, f32[136,128]{1,0:T(8,128)}) custom-call(bf16[2048,1024]{1,0:T(8,128)(2,1)} %get-tuple-element.19.dk_ref, bf16[2048,1024]{1,0:T(8,128)(2,1)} %get-tuple-element.20.dv_ref, bf16[1024,1024]{1,0:T(8,128)(2,1)} %wk_ref.3, bf16[1024,1024]{1,0:T(8,128)(2,1)} %wv_ref.3, f32[136,128]{1,0:T(8,128)} %bitcast.59), custom_call_target="tpu_custom_call" | custom-call | tf_op jit(solution)/shard_map/return_terms/pallas_call | solution.py:526
  210.9 1.5 slice.18
  212.3 1.2 slice.19
  213.6 2.4 %fusion.10 = (f32[256]{0:T(256)S(1)}, f32[256,1024]{1,0:T(8,128)S(1)}) fusion(bf16[1,256,1024]{2,1,0:T(8,128)(2,1)S(1)} %copy-done.2, f32[1024]{0:T(1024)S(1)} %copy-done.10, f32[256,1024]{1,0:T(8,128)} %get-tuple-element.21, bf16[256,1024]{1,0:T(8,128)(2,1)} %get-tuple-element.18, bf16[1024,1024]{1,0:T(8,128)(2,1)S(1)} %copy-done.5), kind=kOutput, calls=%fused_computation.20 | convolution fusion | flops 538181376 | bytes 5248000 | tf_op jit(solution)/shard_map/dot_general | solution.py:37
  216.0 1.2 fusion.11
  (32 shorter events, 0.2 us)
Async XLA Ops:
  7.2 96.1 %copy-start = (bf16[1024,1024]{1,0:T(8,128)(2,1)S(1)}, bf16[1024,1024]{1,0:T(8,128)(2,1)}, u32[]{:S(2)}) copy-start(bf16[1024,1024]{1,0:T(8,128)(2,1)} %param.19) | copy-start | bytes 6291460
  7.2 167.6 %reduce-scatter.4.cloned.1.call-start = ((), (), s32[]{:S(2)}) async-start(), calls=%async_computation.1 | async-start | bytes 626688
  70.3 33.0 %copy-start.1 = (bf16[1,256,1024]{2,1,0:T(8,128)(2,1)S(1)}, bf16[1,256,1024]{2,1,0:T(8,128)(2,1)}, u32[]{:S(2)}) copy-start(bf16[1,256,1024]{2,1,0:T(8,128)(2,1)} %param.11) | copy-start | bytes 1572868
  103.3 2.1 copy-start.6
  103.3 2.1 copy-start.9
  119.2 0.6 copy-start.8
  119.3 2.6 %copy-start.7 = (bf16[1024,128]{1,0:T(8,128)(2,1)S(1)}, bf16[1024,128]{1,0:T(8,128)(2,1)}, u32[]{:S(2)}) copy-start(bf16[1024,128]{1,0:T(8,128)(2,1)} %param.21) | copy-start | bytes 786436
  123.0 1.7 copy-start.3
  174.8 38.8 %copy-start.2 = (bf16[1,256,1024]{2,1,0:T(8,128)(2,1)S(1)}, bf16[1,256,1024]{2,1,0:T(8,128)(2,1)}, u32[]{:S(2)}) copy-start(bf16[1,256,1024]{2,1,0:T(8,128)(2,1)} %param.11) | copy-start | bytes 1572868
  174.8 38.8 %copy-start.5 = (bf16[1024,1024]{1,0:T(8,128)(2,1)S(1)}, bf16[1024,1024]{1,0:T(8,128)(2,1)}, u32[]{:S(2)}) copy-start(bf16[1024,1024]{1,0:T(8,128)(2,1)} %wq_ref.1) | copy-start | bytes 6291460
  174.8 38.8 %copy-start.10 = (f32[1024]{0:T(1024)S(1)}, f32[1024]{0:T(1024)}, u32[]{:S(2)}) copy-start(f32[1024]{0:T(1024)} %param.15) | copy-start | bytes 12292
  213.5 2.4 %copy-start.4 = (f32[256,1024]{1,0:T(8,128)S(1)}, f32[256,1024]{1,0:T(8,128)}, u32[]{:S(2)}) copy-start(f32[256,1024]{1,0:T(8,128)} %copy-done.3) | copy-start | bytes 3145732
  213.6 2.4 %copy-start.11 = (f32[256]{0:T(256)S(1)}, f32[256]{0:T(256)}, u32[]{:S(2)}) copy-start(f32[256]{0:T(256)} %get-tuple-element.29) | copy-start | bytes 3076
Sparse Core Ops, SparseCore 0:
  121.9 32.2 reduce-scatter.3

commit v3 on v2

--- a/solution.py
+++ b/solution.py
@@ -106,72 +106,6 @@
     out_ref[...] = columns.T
     for h in range(heads):
         lse_ref[0, h : h + 1, :] = jnp.log(totals[h])
-
-
-def backward_kernel(
-    head_size,
-    tile,
-    reach_ref,
-    q_ref,
-    k_ref,
-    v_ref,
-    up_ref,
-    mixed_ref,
-    lse_ref,
-    bias_ref,
-    dq_ref,
-    dk_ref,
-    dv_ref,
-):
-    heads = LANES // head_size
-    rows = q_ref.shape[0]
-    scale = 1.0 / math.sqrt(head_size)
-    masks = head_masks(q_ref.shape, 1, heads, head_size)
-    query_heads = masked_heads(q_ref[...], masks, scale)
-    up_heads = masked_heads(up_ref[...], masks, 1.0)
-    product = (up_ref[...].astype(jnp.float32) * mixed_ref[...]).T
-    inner = [
-        jnp.sum(product[h * head_size : (h + 1) * head_size], axis=0, keepdims=True)
-        for h in range(heads)
-    ]
-    lse = [lse_ref[0, h : h + 1, :] for h in range(heads)]
-
-    def clear(block, carry):
-        at = pl.ds(pl.multiple_of(block * tile, tile), tile)
-        dk_ref[at, :] = jnp.zeros((tile, LANES), jnp.bfloat16)
-        dv_ref[at, :] = jnp.zeros((tile, LANES), jnp.bfloat16)
-        return carry
-
-    lax.fori_loop(0, reach_ref[0], clear, 0)
-    lax.fori_loop(reach_ref[1], k_ref.shape[0] // tile, clear, 0)
-
-    def step(block, grads):
-        at = pl.ds(pl.multiple_of(block * tile, tile), tile)
-        keys = k_ref[at, :]
-        values = v_ref[at, :]
-        bias = bias_ref[at, :]
-        key_sum = jnp.zeros((tile, LANES), jnp.float32)
-        value_sum = jnp.zeros((tile, LANES), jnp.float32)
-        new = []
-        for h in range(heads):
-            soft = jnp.exp(dot_last(keys, query_heads[h]) + (bias - lse[h]))
-            d_soft = dot_last(values, up_heads[h])
-            d_score = (soft * (d_soft - inner[h])).astype(jnp.bfloat16)
-            key_sum += jnp.dot(d_score, query_heads[h], preferred_element_type=jnp.float32)
-            value_sum += jnp.dot(
-                soft.astype(jnp.bfloat16), up_heads[h], preferred_element_type=jnp.float32
-            )
-            new.append(grads[h] + dot_first(keys, d_score))
-        dk_ref[at, :] = key_sum.astype(jnp.bfloat16)
-        dv_ref[at, :] = value_sum.astype(jnp.bfloat16)
-        return tuple(new)
-
-    zero = tuple(jnp.zeros((LANES, rows), jnp.float32) for _ in range(heads))
-    grads = lax.fori_loop(reach_ref[0], reach_ref[1], step, zero)
-    columns = jnp.concatenate(
-        [grads[h][h * head_size : (h + 1) * head_size] for h in range(heads)], axis=0
-    )
-    dq_ref[...] = (columns * scale).T.astype(jnp.bfloat16)
 
 
 def attention_forward(queries, key_rows, value_rows, bias, reach):
@@ -202,37 +136,6 @@
         compiler_params=pltpu.CompilerParams(vmem_limit_bytes=VMEM_BYTES),
         name="attention_forward",
     )(reach, queries, key_rows, value_rows, bias)
-
-
-def attention_backward(queries, key_rows, value_rows, upstream, mixed, lse, bias, reach):
-    rows, model_width = queries.shape
-    slots = key_rows.shape[0]
-    head_size = model_width // HEADS
-    heads = LANES // head_size
-    row_spec = pl.BlockSpec((rows, LANES), lambda i: (0, i))
-    slot_spec = pl.BlockSpec((slots, LANES), lambda i: (0, i))
-    return pl.pallas_call(
-        functools.partial(backward_kernel, head_size, rows),
-        grid=(model_width // LANES,),
-        in_specs=[
-            pl.BlockSpec(memory_space=pltpu.SMEM),
-            row_spec,
-            slot_spec,
-            slot_spec,
-            row_spec,
-            row_spec,
-            pl.BlockSpec((1, heads, rows), lambda i: (i, 0, 0)),
-            pl.BlockSpec((slots, rows), lambda i: (0, 0)),
-        ],
-        out_specs=[row_spec, slot_spec, slot_spec],
-        out_shape=[
-            jax.ShapeDtypeStruct((rows, model_width), jnp.bfloat16),
-            jax.ShapeDtypeStruct((slots, model_width), jnp.bfloat16),
-            jax.ShapeDtypeStruct((slots, model_width), jnp.bfloat16),
-        ],
-        compiler_params=pltpu.CompilerParams(vmem_limit_bytes=VMEM_BYTES),
-        name="attention_backward",
-    )(reach, queries, key_rows, value_rows, upstream, mixed, lse, bias)
 
 
 MESH = pl.DeviceIdType.MESH
@@ -308,44 +211,43 @@
     order = far_first(pairs)
     targets = {d: (member, 2 * partner(pair, d) + core) for d in order}
     greet([sibling] + [targets[d] for d in order])
+    own = pl.ds(pl.multiple_of(band * slots, slots), slots)
     copies = {
-        d: send(normed_ref, held.at[band], send_sem.at[d], recv_sem.at[d], targets[d])
+        d: send(normed_ref, held.at[own], send_sem.at[d], recv_sem.at[d], targets[d])
         for d in order
     }
-    copies[0] = send(normed_ref, held.at[band], send_sem.at[0], recv_sem.at[0], sibling)
+    copies[0] = send(normed_ref, held.at[own], send_sem.at[0], recv_sem.at[0], sibling)
     for d in order + [0]:
         copies[d].start()
     first = jnp.clip(band - HOPS, 0, bands - window)
 
-    def project(rows_ref, source):
-        def run():
-            place = pl.ds(pl.multiple_of((source - first) * slots, slots), slots)
-            project_into(rows_ref, wk_ref, k_ref.at[place])
-            project_into(rows_ref, wv_ref, v_ref.at[place])
-
+    def project(source, count):
+        rows = pl.ds(pl.multiple_of(source * slots, slots), count * slots)
+        place = pl.ds(pl.multiple_of((source - first) * slots, slots), count * slots)
+        project_into(held.at[rows], wk_ref, k_ref.at[place])
+        project_into(held.at[rows], wv_ref, v_ref.at[place])
+
+    def project_pair(source_pair):
         if window == bands:
-            run()
+            project(2 * source_pair, 2)
         else:
-            pl.when((source >= first) & (source < first + window))(run)
-
+            for source in (2 * source_pair, 2 * source_pair + 1):
+                inside = (source >= first) & (source < first + window)
+                pl.when(inside)(functools.partial(project, source, 1))
+
+    held[own, :] = normed_ref[...]
     project_into(normed_ref, wq_ref, q_ref)
-    project(normed_ref, band)
     copies[0].wait_recv()
-    project(held.at[2 * pair + 1 - core], 2 * pair + 1 - core)
+    project_pair(pair)
     passes = {}
-    near_first = order[::-1]
-    for d in near_first:
+    for d in order[::-1]:
         copies[d].wait_recv()
         source = 2 * partner(pair, d) + core
-        passes[d] = send(
-            held.at[source], held.at[source], pass_send.at[d], pass_recv.at[d], sibling
-        )
+        rows = pl.ds(pl.multiple_of(source * slots, slots), slots)
+        passes[d] = send(held.at[rows], held.at[rows], pass_send.at[d], pass_recv.at[d], sibling)
         passes[d].start()
-        project(held.at[source], source)
-    for d in near_first:
         passes[d].wait_recv()
-        source = 2 * partner(pair, d) + 1 - core
-        project(held.at[source], source)
+        project_pair(partner(pair, d))
     for d in order + [0]:
         copies[d].wait_send()
     for d in order:
@@ -366,7 +268,7 @@
             jax.ShapeDtypeStruct((window * slots, model_width), jnp.bfloat16),
         ],
         scratch_shapes=[
-            pltpu.VMEM((bands, slots, model_width), jnp.bfloat16),
+            pltpu.VMEM((bands * slots, model_width), jnp.bfloat16),
             pltpu.SemaphoreType.DMA((pairs,)),
             pltpu.SemaphoreType.DMA((pairs,)),
             pltpu.SemaphoreType.DMA((pairs,)),
@@ -418,77 +320,142 @@
     )(own)
 
 
-def terms_kernel(
+def backward_kernel(
     bands,
     members,
-    window,
-    dk_ref,
-    dv_ref,
+    head_size,
+    q_ref,
+    k_ref,
+    v_ref,
+    up_ref,
+    mixed_ref,
+    lse_ref,
+    bias_ref,
     wk_ref,
     wv_ref,
     head_ref,
+    dq_ref,
     total_ref,
     head_out,
+    dq_sum,
+    query_held,
+    up_held,
+    inner_held,
+    dk_held,
+    dv_held,
     for_sibling,
     from_sibling,
     outgoing,
     arriving,
-    head_held,
+    head_bands,
+    head_own,
+    head_members,
     sib_send,
     sib_recv,
     far_send,
     far_recv,
+    band_send,
+    band_recv,
     head_send,
     head_recv,
 ):
     member, band, pair, core = band_layout()
     pairs = bands // 2
     slots = total_ref.shape[0]
+    window = k_ref.shape[0] // slots
+    steps = q_ref.shape[1] // LANES
+    heads = LANES // head_size
+    scale = 1.0 / math.sqrt(head_size)
     sibling = (member, 2 * pair + 1 - core)
     order = far_first(pairs)
     targets = {d: (member, 2 * partner(pair, d) + core) for d in order}
     others = member_targets(members)
-    greet([sibling] + [targets[d] for d in order] + others)
-    head_copies = [
-        send(head_ref, head_held.at[member], head_send.at[d], head_recv.at[d], others[d])
-        for d in range(members - 1)
+    ring = [lax.rem(band + d, bands) for d in range(1, bands)]
+    greet([(member, other) for other in ring] + others)
+    band_copies = [
+        send(
+            head_ref.at[other],
+            head_bands.at[band],
+            band_send.at[d],
+            band_recv.at[d],
+            (member, other),
+        )
+        for d, other in enumerate(ring)
     ]
-    for copy in head_copies:
+    for copy in band_copies:
         copy.start()
+    head_bands[band] = head_ref[band]
     first = jnp.clip(band - HOPS, 0, bands - window)
-
-    def project(target, out_ref):
-        def run():
+    masks = head_masks((slots, LANES), 1, heads, head_size)
+
+    @pl.loop(0, steps)
+    def _(i):
+        lanes = pl.ds(pl.multiple_of(i * LANES, LANES), LANES)
+        up = up_ref[:, lanes]
+        product = (up.astype(jnp.float32) * mixed_ref[:, lanes]).T
+        query_heads = masked_heads(q_ref[:, lanes], masks, scale)
+        up_heads = masked_heads(up, masks, 1.0)
+        for h in range(heads):
+            query_held[i, h] = query_heads[h]
+            up_held[i, h] = up_heads[h]
+            inner_held[i, h : h + 1, :] = jnp.sum(
+                product[h * head_size : (h + 1) * head_size], axis=0, keepdims=True
+            )
+        dq_sum[i] = jnp.zeros((LANES, slots), jnp.float32)
+
+    def terms_of(target, out_ref):
+        inside = (target - band <= HOPS) & (band - target <= HOPS)
+
+        @pl.when(inside)
+        def _():
             place = pl.ds(pl.multiple_of((target - first) * slots, slots), slots)
+
+            @pl.loop(0, steps)
+            def _(i):
+                lanes = pl.ds(pl.multiple_of(i * LANES, LANES), LANES)
+                keys = k_ref[place, lanes]
+                values = v_ref[place, lanes]
+                bias = bias_ref[place, :]
+                key_sum = jnp.zeros((slots, LANES), jnp.float32)
+                value_sum = jnp.zeros((slots, LANES), jnp.float32)
+                for h in range(heads):
+                    query = query_held[i, h]
+                    up = up_held[i, h]
+                    soft = jnp.exp(dot_last(keys, query) + (bias - lse_ref[i, h : h + 1, :]))
+                    d_soft = dot_last(values, up)
+                    d_score = (soft * (d_soft - inner_held[i, h : h + 1, :])).astype(jnp.bfloat16)
+                    key_sum += jnp.dot(d_score, query, preferred_element_type=jnp.float32)
+                    value_sum += jnp.dot(
+                        soft.astype(jnp.bfloat16), up, preferred_element_type=jnp.float32
+                    )
+                    part = pl.ds(h * head_size, head_size)
+                    dq_sum[i, part, :] += dot_first(keys, d_score)[
+                        h * head_size : (h + 1) * head_size
+                    ]
+                dk_held[:, lanes] = key_sum.astype(jnp.bfloat16)
+                dv_held[:, lanes] = value_sum.astype(jnp.bfloat16)
 
             @pl.loop(0, wk_ref.shape[0] // COLUMNS)
             def _(tile):
                 at = pl.ds(pl.multiple_of(tile * COLUMNS, COLUMNS), COLUMNS)
                 out_ref[:, at] = (
-                    dot_last(dk_ref[place, :], wk_ref[at, :])
-                    + dot_last(dv_ref[place, :], wv_ref[at, :])
+                    dot_last(dk_held[...], wk_ref[at, :]) + dot_last(dv_held[...], wv_ref[at, :])
                 ).astype(out_ref.dtype)
 
-        if window == bands:
-            run()
-        else:
-            inside = (target >= first) & (target < first + window)
-            pl.when(inside)(run)
-
-            @pl.when(jnp.logical_not(inside))
-            def _():
-                out_ref[...] = jnp.zeros(out_ref.shape, out_ref.dtype)
+        @pl.when(jnp.logical_not(inside))
+        def _():
+            out_ref[...] = jnp.zeros(out_ref.shape, out_ref.dtype)
 
     near = {}
     far = {}
     for d in order + [0]:
         there = partner(pair, d)
-        project(2 * there + 1 - core, for_sibling.at[d])
+        terms_of(2 * there + 1 - core, for_sibling.at[d])
         near[d] = send(
             for_sibling.at[d], from_sibling.at[d], sib_send.at[d], sib_recv.at[d], sibling
         )
         near[d].start()
-        project(2 * there + core, outgoing.at[d])
+        terms_of(2 * there + core, outgoing.at[d])
         near[d].wait_recv()
         if d:
             outgoing[d] = (
@@ -500,12 +467,33 @@
             far[d].start()
         else:
             total_ref[...] = outgoing[0].astype(jnp.float32) + from_sibling[0].astype(jnp.float32)
-    head_held[member] = head_ref[...]
+        if d == order[-1]:
+            for copy in band_copies:
+                copy.wait_recv()
+            head_sum = head_bands[0]
+            for other in range(1, bands):
+                head_sum += head_bands[other]
+            head_own[...] = head_sum
+            head_copies = [
+                send(
+                    head_own, head_members.at[member], head_send.at[e], head_recv.at[e], others[e]
+                )
+                for e in range(members - 1)
+            ]
+            for copy in head_copies:
+                copy.start()
+            head_members[member] = head_sum
+
+    @pl.loop(0, steps)
+    def _(i):
+        lanes = pl.ds(pl.multiple_of(i * LANES, LANES), LANES)
+        dq_ref[:, lanes] = (dq_sum[i] * scale).T.astype(jnp.bfloat16)
+
     for copy in head_copies:
         copy.wait_recv()
-    head_sum = head_held[0]
+    head_sum = head_members[0]
     for other in range(1, members):
-        head_sum += head_held[other]
+        head_sum += head_members[other]
     head_out[...] = head_sum
     for d in order:
         far[d].wait_recv()
@@ -514,41 +502,60 @@
         far[d].wait_send()
         near[d].wait_send()
     near[0].wait_send()
-    for copy in head_copies:
+    for copy in band_copies + head_copies:
         copy.wait_send()
 
 
-def project_and_return(key_terms, value_terms, w_key, w_value, head, bands, members, window):
-    slots, model_width = key_terms.shape[0] // window, key_terms.shape[1]
+def attention_backward(
+    queries, key_rows, value_rows, upstream, mixed, lse, bias, w_key, w_value, head, members
+):
+    slots, model_width = queries.shape
+    bands, head_rows, channels = head.shape
+    head_size = model_width // HEADS
+    heads = LANES // head_size
+    steps = model_width // LANES
     vmem = pl.BlockSpec(memory_space=pltpu.VMEM)
     pairs = bands // 2
     blocks = pltpu.VMEM((pairs, slots, model_width), jnp.bfloat16)
+    rows = pltpu.VMEM((slots, model_width), jnp.bfloat16)
+    masked = pltpu.VMEM((steps, heads, slots, LANES), jnp.bfloat16)
     return pl.pallas_call(
-        functools.partial(terms_kernel, bands, members, window),
-        in_specs=[vmem] * 5,
-        out_specs=[vmem] * 2,
+        functools.partial(backward_kernel, bands, members, head_size),
+        in_specs=[vmem] * 10,
+        out_specs=[vmem] * 3,
         out_shape=[
+            jax.ShapeDtypeStruct((slots, model_width), jnp.bfloat16),
             jax.ShapeDtypeStruct((slots, model_width), jnp.float32),
-            jax.ShapeDtypeStruct(head.shape, jnp.float32),
+            jax.ShapeDtypeStruct((head_rows, channels), jnp.float32),
         ],
         scratch_shapes=[
+            pltpu.VMEM((steps, LANES, slots), jnp.float32),
+            masked,
+            masked,
+            pltpu.VMEM((steps, heads, slots), jnp.float32),
+            rows,
+            rows,
             blocks,
             blocks,
             blocks,
             blocks,
-            pltpu.VMEM((members,) + head.shape, jnp.float32),
-            pltpu.SemaphoreType.DMA((pairs,)),
-            pltpu.SemaphoreType.DMA((pairs,)),
-            pltpu.SemaphoreType.DMA((pairs,)),
-            pltpu.SemaphoreType.DMA((pairs,)),
+            pltpu.VMEM((bands, head_rows, channels), jnp.float32),
+            pltpu.VMEM((head_rows, channels), jnp.float32),
+            pltpu.VMEM((members, head_rows, channels), jnp.float32),
+            pltpu.SemaphoreType.DMA((pairs,)),
+            pltpu.SemaphoreType.DMA((pairs,)),
+            pltpu.SemaphoreType.DMA((pairs,)),
+            pltpu.SemaphoreType.DMA((pairs,)),
+            pltpu.SemaphoreType.DMA((bands - 1,)),
+            pltpu.SemaphoreType.DMA((bands - 1,)),
             pltpu.SemaphoreType.DMA((members - 1,)),
             pltpu.SemaphoreType.DMA((members - 1,)),
         ],
         compiler_params=pltpu.CompilerParams(
             collective_id=2, has_side_effects=True, vmem_limit_bytes=VMEM_BYTES
         ),
-        name="return_terms",
-    )(key_terms, value_terms, w_key, w_value, head)
+        name="attention_backward",
+    )(queries, key_rows, value_rows, upstream, mixed, lse, bias, w_key, w_value, head)
 
 
 def own_accuracy(own, others, measured, weight):
@@ -646,12 +653,18 @@
     head_part = dot_first(head_in, grad_pred).reshape(bands, model_width // bands, channels)
     loss_rows = jnp.broadcast_to(loss_part, (bands, 8, channels))
     packed = jnp.concatenate([head_part, loss_rows], axis=1)
-    packed = lax.psum_scatter(packed, "band", scatter_dimension=0, tiled=False)
-    grad_queries, key_terms, value_terms = attention_backward(
-        queries, key_rows, value_rows, grad_mixed, mixed, lse, bias, reach
-    )
-    normed_total, packed = project_and_return(
-        key_terms, value_terms, w_key, w_value, packed, bands, members, window
+    grad_queries, normed_total, packed = attention_backward(
+        queries,
+        key_rows,
+        value_rows,
+        grad_mixed,
+        mixed,
+        lse,
+        bias,
+        w_key,
+        w_value,
+        packed,
+        members,
     )
     grad_head = packed[: model_width // bands]
     ensemble_loss = packed[model_width // bands, 0]

time: 228 us -> 196 us (0.86)
  Pallas kernels: 174 us -> 159 us
  between operations: 16.2 us -> 2.75 us
    pallas_call x2 -> x1, Pallas kernels: 86.1 us -> 73.3 us  [attention_backward(): pl.pallas_call(functools.partial(backward_kernel, bands, members, head_si...]
    pallas_call x1, Pallas kernels: 33 us -> 29.7 us  [attention_forward(): pl.pallas_call(functools.partial(forward_kernel, head_size, rows), grid=(...]
  transfers between devices with their start and end apart: 1 -> 0, of which waited for: 0 -> 0; matrix products, arithmetic and copies ran while one was open for 1% -> 0% of each run, Pallas kernels for 22% -> 0%
where the time goes in v3:
time: 196 us; the launch traced here: 192 us
  Pallas kernels  159 us (81%)
  other arithmetic  17.4 us (9%)
  matrix products  7.73 us (4%)
  local copies, waits for them, and re-layouts  5.41 us (3%)
  between operations  2.75 us (1%)
    pallas_call x1, Pallas kernels, attention_backward(): pl.pallas_call(functools.partial(backward_kernel, bands, members, head_si...  73.3 us
    pallas_call x1, Pallas kernels, gather_and_project(): pl.pallas_call(functools.partial(gather_kernel, bands, window), in_specs=...  48.1 us
    pallas_call x1, Pallas kernels, attention_forward(): pl.pallas_call(functools.partial(forward_kernel, head_size, rows), grid=(...  29.7 us
    pallas_call x1, Pallas kernels, exchange_members(): pl.pallas_call(functools.partial(exchange_kernel, members), in_specs=[vme...  8.11 us
    dot_general x3, matrix products, times_transposed(): lax.dot_general(left_side, scaling_coefficient, (((left_side.ndim - 1,),...  4.25 us

profile of v3, /device:TPU:3, one launch (start us, length us, event | category | flops | bytes accessed | tf_op | source)
XLA Modules:
  0.0 192.5 jit_solution(1825981737954972920)
XLA Ops:
  0.6 0.0 copy-start
  0.7 1.4 dynamic_slice.9
  2.0 0.8 reduce-window.9
  2.9 1.2 fusion.3
  4.1 1.3 fusion.17
  6.1 0.6 dynamic_slice.8
  8.0 1.3 fusion.15
  9.3 0.7 iota_add_fusion
  10.0 0.6 select_reduce_fusion.1
  10.6 1.9 %pad_add_fusion.reach_ref = s32[2]{0:T(128)} fusion(s32[1]{0:T(128)} %bitcast.5, s32[1]{0:T(128)} %bitcast.4), kind=kLoop, calls=%fused_computation.52 | loop fusion | flops 2 | bytes 16 | tf_op jit(solution)/shard_map/stack | solution.py:626
  12.5 0.7 fusion.14
  13.3 0.1 add_bitcast_fusion
  13.4 2.0 %fusion.5.normed_ref = bf16[256,1024]{1,0:T(8,128)(2,1)} fusion(bf16[1,256,1024]{2,1,0:T(8,128)(2,1)} %param.11, f32[1024]{0:T(1024)} %param.15, f32[256]{0:T(256)S(1)} %get-tuple-element.26), kind=kLoop, calls=%fused_computation.15 | loop fusion | flops 1048576 | bytes 1053696 | tf_op jit(solution)/shard_map/convert_element_type | solution.py:601
  15.4 2.7 %fusion.1.bias_ref = f32[2048,256]{1,0:T(8,128)} fusion(s32[256]{0:T(256)S(1)} %iota_add_fusion, s32[2048]{0:T(1024)S(1)} %bitcast.57, pred[2048]{0:T(1024)(128)(4,1)S(1)} %and.34), kind=kLoop, calls=%fused_computation.7 | loop fusion | flops 2621440 | bytes 2108416 | tf_op jit(solution)/shard_map/jit(_where)/select_n | solution.py:619
  18.1 48.1 %gather_rows.1 = (bf16[256,1024]{1,0:T(8,128)(2,1)}, bf16[2048,1024]{1,0:T(8,128)(2,1)}, bf16[2048,1024]{1,0:T(8,128)(2,1)}) custom-call(bf16[256,1024]{1,0:T(8,128)(2,1)} %fusion.5.normed_ref, bf16[1024,1024]{1,0:T(8,128)(2,1)} %wq_ref.1, bf16[1024,1024]{1,0:T(8,128)(2,1)} %wk_ref.3, bf16[1024,1024]{1,0:T(8,128)(2,1)} %wv_ref.3), custom_call_target="tpu_custom_call" | custom-call | tf_op jit(solution)/shard_map/gather_rows/pallas_call | solution.py:261
  66.2 0.0 copy-start.1
  66.3 29.7 %attention_forward.1 = (f32[256,1024]{1,0:T(8,128)}, f32[8,2,256]{2,1,0:T(2,128)}) custom-call(s32[2]{0:T(128)} %pad_add_fusion.reach_ref, bf16[256,1024]{1,0:T(8,128)(2,1)} %get-tuple-element.11.q_ref, bf16[2048,1024]{1,0:T(8,128)(2,1)} %get-tuple-element.12.k_ref, bf16[2048,1024]{1,0:T(8,128)(2,1)} %get-tuple-element.13.v_ref, f32[2048,256]{1,0:T(8,128)} %fusion.1.bias_ref), custom_call_target="tpu_custom_call" | custom-call | tf_op jit(solution)/shard_map/attention_forward/pallas_call | solution.py:117
  95.9 0.0 copy-start.4
  96.0 2.1 %multiply_reduce_fusion.1 = (f32[256]{0:T(256)S(1)}, f32[256,1024]{1,0:T(8,128)S(1)}) fusion(bf16[1024,1024]{1,0:T(8,128)(2,1)S(1)} %copy-done, f32[256,1024]{1,0:T(8,128)} %get-tuple-element.14.mixed_ref, bf16[1,256,1024]{2,1,0:T(8,128)(2,1)S(1)} %copy-done.1), kind=kOutput, calls=%fused_computation.24 | convolution fusion | flops 538181376 | bytes 4719616 | tf_op jit(solution)/shard_map/dot_general | solution.py:634
  98.1 1.0 convolution_convert_fusion.1.own_ref
  99.1 8.1 %exchange_members.1 = bf16[3,256,128]{2,1,0:T(8,128)(2,1)} custom-call(bf16[256,128]{1,0:T(8,128)(2,1)} %convolution_convert_fusion.1.own_ref), custom_call_target="tpu_custom_call" | custom-call | tf_op jit(solution)/shard_map/exchange_members/pallas_call | solution.py:308
  107.2 1.0 convert_element_type.52
  108.2 1.7 multiply_reduce_fusion.2
  109.9 0.4 fusion.16
  110.3 1.5 concatenate.3.head_ref
  111.8 0.4 multiply_reduce_fusion
  112.2 1.6 convolution_convert_fusion.up_ref
  113.8 73.3 %attention_backward.1 = (bf16[256,1024]{1,0:T(8,128)(2,1)}, f32[256,1024]{1,0:T(8,128)}, f32[136,128]{1,0:T(8,128)}) custom-call(bf16[256,1024]{1,0:T(8,128)(2,1)} %get-tuple-element.11.q_ref, bf16[2048,1024]{1,0:T(8,128)(2,1)} %get-tuple-element.12.k_ref, bf16[2048,1024]{1,0:T(8,128)(2,1)} %get-tuple-element.13.v_ref, ...), custom_call_target="tpu_custom_call" | custom-call | tf_op jit(solution)/shard_map/attention_backward/pallas_call | solution.py:522
  187.1 1.2 slice.19
  188.3 2.3 %fusion.10 = (f32[256]{0:T(256)S(1)}, f32[256,1024]{1,0:T(8,128)S(1)}) fusion(bf16[1,256,1024]{2,1,0:T(8,128)(2,1)S(1)} %copy-done.2, f32[1024]{0:T(1024)S(1)} %copy-done.8, f32[256,1024]{1,0:T(8,128)} %get-tuple-element.17, bf16[256,1024]{1,0:T(8,128)(2,1)} %get-tuple-element.16, bf16[1024,1024]{1,0:T(8,128)(2,1)S(1)} %copy-done.3), kind=kOutput, calls=%fused_computation.20 | convolution fusion | flops 538181376 | bytes 5248000 | tf_op jit(solution)/shard_map/dot_general | solution.py:37
  190.6 1.2 fusion.11
  191.9 0.6 slice.18
  (22 shorter events, 0.1 us)
Async XLA Ops:
  0.6 95.3 %copy-start = (bf16[1024,1024]{1,0:T(8,128)(2,1)S(1)}, bf16[1024,1024]{1,0:T(8,128)(2,1)}, u32[]{:S(2)}) copy-start(bf16[1024,1024]{1,0:T(8,128)(2,1)} %param.19) | copy-start | bytes 6291460
  66.2 29.7 %copy-start.1 = (bf16[1,256,1024]{2,1,0:T(8,128)(2,1)S(1)}, bf16[1,256,1024]{2,1,0:T(8,128)(2,1)}, u32[]{:S(2)}) copy-start(bf16[1,256,1024]{2,1,0:T(8,128)(2,1)} %param.11) | copy-start | bytes 1572868
  95.9 2.1 %copy-start.4 = (bf16[1024,128]{1,0:T(8,128)(2,1)S(1)}, bf16[1024,128]{1,0:T(8,128)(2,1)}, u32[]{:S(2)}) copy-start(bf16[1024,128]{1,0:T(8,128)(2,1)} %param.21) | copy-start | bytes 786436
  96.0 2.1 %copy-start.7 = (f32[1024]{0:T(1024)S(1)}, f32[1024]{0:T(1024)}, u32[]{:S(2)}) copy-start(f32[1024]{0:T(1024)} %param.20) | copy-start | bytes 12292
  98.0 10.1 %copy-start.5 = (bf16[256,128]{1,0:T(8,128)(2,1)S(1)}, bf16[256,128]{1,0:T(8,128)(2,1)}, u32[]{:S(2)}) copy-start(bf16[256,128]{1,0:T(8,128)(2,1)} %param.12) | copy-start | bytes 196612
  113.8 74.5 %copy-start.2 = (bf16[1,256,1024]{2,1,0:T(8,128)(2,1)S(1)}, bf16[1,256,1024]{2,1,0:T(8,128)(2,1)}, u32[]{:S(2)}) copy-start(bf16[1,256,1024]{2,1,0:T(8,128)(2,1)} %param.11) | copy-start | bytes 1572868
  113.8 74.5 %copy-start.3 = (bf16[1024,1024]{1,0:T(8,128)(2,1)S(1)}, bf16[1024,1024]{1,0:T(8,128)(2,1)}, u32[]{:S(2)}) copy-start(bf16[1024,1024]{1,0:T(8,128)(2,1)} %wq_ref.1) | copy-start | bytes 6291460
  113.8 74.5 %copy-start.8 = (f32[1024]{0:T(1024)S(1)}, f32[1024]{0:T(1024)}, u32[]{:S(2)}) copy-start(f32[1024]{0:T(1024)} %param.15) | copy-start | bytes 12292
  190.6 1.2 copy-start.6

commit v4 on v3

--- a/solution.py
+++ b/solution.py
@@ -186,6 +186,70 @@
         out_ref[:, at] = jnp.dot(
             rows_ref[...], weight_ref[:, at], preferred_element_type=jnp.float32
         ).astype(out_ref.dtype)
+
+
+def write_mask(bands, window, band, first, slots, counts_ref, bias_ref, reach_ref):
+    own_first = jnp.int32(0)
+    start = jnp.int32(0)
+    for b in range(bands):
+        own_first += jnp.where(b < band, counts_ref[b], 0)
+        start += jnp.where(b < first, counts_ref[b], 0)
+    key_slot = lax.broadcasted_iota(jnp.int32, (slots, slots), 0)
+    query_slot = lax.broadcasted_iota(jnp.int32, (slots, slots), 1)
+
+    def one_band(w, carry):
+        low, high, start = carry
+        count = counts_ref[first + w]
+        within = jnp.abs(first + w - band) <= HOPS
+        live = key_slot < jnp.where(within, count, 0)
+        gap = (key_slot - query_slot) + (start - own_first)
+        place = pl.ds(pl.multiple_of(w * slots, slots), slots)
+        bias_ref[place, :] = jnp.where(live & (jnp.abs(gap) <= R), 0.0, MASKED)
+        reached = (
+            within
+            & (start <= own_first + (slots - 1) + R)
+            & (start + count - 1 >= own_first - R)
+        )
+        low = jnp.minimum(low, jnp.where(reached, w, window))
+        high = jnp.maximum(high, jnp.where(reached, w + 1, 0))
+        return low, high, start + count
+
+    low, high, _ = lax.fori_loop(
+        0, window, one_band, (jnp.int32(window), jnp.int32(0), start)
+    )
+    reach_ref[0] = low
+    reach_ref[1] = high
+
+
+def prepare_kernel(
+    bands, window, counts_ref, latent_ref, gain_ref, normed_ref, bias_ref, inverse_ref, reach_ref
+):
+    band = lax.axis_index("band")
+    first = jnp.clip(band - HOPS, 0, bands - window)
+    latent = latent_ref[...].astype(jnp.float32)
+    inverse = inverse_rms(latent)
+    inverse_ref[...] = inverse
+    normed_ref[...] = (latent * inverse * gain_ref[...]).astype(jnp.bfloat16)
+    write_mask(bands, window, band, first, latent.shape[0], counts_ref, bias_ref, reach_ref)
+
+
+def prepare_rows(band_counts, latent, gain, bands, window):
+    slots, model_width = latent.shape
+    vmem = pl.BlockSpec(memory_space=pltpu.VMEM)
+    smem = pl.BlockSpec(memory_space=pltpu.SMEM)
+    return pl.pallas_call(
+        functools.partial(prepare_kernel, bands, window),
+        in_specs=[smem, vmem, vmem],
+        out_specs=[vmem, vmem, vmem, smem],
+        out_shape=[
+            jax.ShapeDtypeStruct((slots, model_width), jnp.bfloat16),
+            jax.ShapeDtypeStruct((window * slots, slots), jnp.float32),
+            jax.ShapeDtypeStruct((slots, 1), jnp.float32),
+            jax.ShapeDtypeStruct((2,), jnp.int32),
+        ],
+        compiler_params=pltpu.CompilerParams(vmem_limit_bytes=VMEM_BYTES),
+        name="prepare_rows",
+    )(band_counts, latent, gain)
 
 
 def gather_kernel(
@@ -217,7 +281,7 @@
         for d in order
     }
     copies[0] = send(normed_ref, held.at[own], send_sem.at[0], recv_sem.at[0], sibling)
-    for d in order + [0]:
+    for d in [0] + order[::-1]:
         copies[d].start()
     first = jnp.clip(band - HOPS, 0, bands - window)
 
@@ -594,41 +658,15 @@
     _, slots, model_width = latent.shape
     channels = w_head.shape[1]
     window = min(bands, 2 * HOPS + 1)
-    first_band = jnp.clip(band - HOPS, 0, bands - window)
 
     latent_f = latent[0].astype(jnp.float32)
-    inverse_one = inverse_rms(latent_f)
-    normed = (latent_f * inverse_one * gain_attn).astype(jnp.bfloat16)
+    normed, bias, inverse_one, reach = prepare_rows(
+        band_counts, latent[0], gain_attn[None], bands, window
+    )
     queries, key_rows, value_rows = gather_and_project(
         normed, w_query, w_key, w_value, bands, window
     )
-
-    slot_iota = jnp.arange(slots, dtype=jnp.int32)
-    offsets = jnp.cumsum(band_counts) - band_counts
-    own_first = offsets[band]
-    own_pos = own_first + slot_iota
-    own_live = slot_iota < band_counts[band]
-    near = first_band + jnp.arange(window, dtype=jnp.int32)
-    near_first = lax.dynamic_slice_in_dim(offsets, first_band, window, 0)
-    near_count = lax.dynamic_slice_in_dim(band_counts, first_band, window, 0)
-    within = jnp.abs(near - band) <= HOPS
-    key_pos = near_first[:, None] + slot_iota[None, :]
-    key_live = (slot_iota[None, :] < near_count[:, None]) & within[:, None]
-    key_pos = key_pos.reshape(-1)
-    allowed = key_live.reshape(-1)[:, None] & (jnp.abs(key_pos[:, None] - own_pos[None, :]) <= R)
-    bias = jnp.where(allowed, 0.0, MASKED).astype(jnp.float32)
-    reached = (
-        within
-        & (near_first <= own_first + (slots - 1) + R)
-        & (near_first + near_count - 1 >= own_first - R)
-    )
-    index = jnp.arange(window, dtype=jnp.int32)
-    reach = jnp.stack(
-        [
-            jnp.min(jnp.where(reached, index, window)),
-            jnp.max(jnp.where(reached, index + 1, 0)),
-        ]
-    ).astype(jnp.int32)
+    own_live = jnp.arange(slots, dtype=jnp.int32) < band_counts[band]
 
     mixed, lse = attention_forward(queries, key_rows, value_rows, bias, reach)
     hidden = latent_f + jnp.dot(

time: 196 us -> 176 us (0.90); the launches traced: 192 us -> 177 us
  other arithmetic: 17.4 us -> 7.75 us
  Pallas kernels: 159 us -> 156 us
    pallas_call x1, Pallas kernels: 48.1 us -> 38.2 us  [gather_and_project(): pl.pallas_call(functools.partial(gather_kernel, bands, window), in_specs=...]
    pallas_call x1, Pallas kernels: 29.7 us -> 33 us  [attention_forward(): pl.pallas_call(functools.partial(forward_kernel, head_size, rows), grid=(...]
    pallas_call x0 -> x1, Pallas kernels: none -> 3.31 us  [prepare_rows(): pl.pallas_call(functools.partial(prepare_kernel, bands, window), in_specs...]
    another operation x2 -> x0, other arithmetic: 2.77 us -> none  [the longest x1 1.94 us: body(): jnp.stack([jnp.min(jnp.where(reached, index, window)), jnp.max(jnp.where(...]
    select_n x1 -> x0, other arithmetic: 2.71 us -> none  [body(): bias = jnp.where(allowed, 0.0, MASKED).astype(jnp.float32)]
    convert_element_type x1 -> x0, other arithmetic: 2.02 us -> none  [body(): normed = (latent_f * inverse_one * gain_attn).astype(jnp.bfloat16)]
where the time goes in v4:
time: 176 us; the launch traced here: 177 us
  Pallas kernels  156 us (89%)
  other arithmetic  7.75 us (4%)
  matrix products  7.73 us (4%)
  local copies, waits for them, and re-layouts  4.66 us (3%)
    pallas_call x1, Pallas kernels, attention_backward(): pl.pallas_call(functools.partial(backward_kernel, bands, members, head_si...  73.3 us
    pallas_call x1, Pallas kernels, gather_and_project(): pl.pallas_call(functools.partial(gather_kernel, bands, window), in_specs=...  38.2 us
    pallas_call x1, Pallas kernels, attention_forward(): pl.pallas_call(functools.partial(forward_kernel, head_size, rows), grid=(...  33 us
    pallas_call x1, Pallas kernels, exchange_members(): pl.pallas_call(functools.partial(exchange_kernel, members), in_specs=[vme...  8.13 us
    dot_general x3, matrix products, times_transposed(): lax.dot_general(left_side, scaling_coefficient, (((left_side.ndim - 1,),...  4.26 us

profile of v4, /device:TPU:3, one launch (start us, length us, event | category | flops | bytes accessed | tf_op | source)
XLA Modules:
  0.0 177.5 jit_solution(5525959840144987937)
XLA Ops:
  0.6 0.0 copy-start
  0.6 1.4 reduce_sum.46
  2.7 1.2 dynamic_slice.3
  4.0 1.3 fusion.10
  5.3 3.3 %prepare_rows.1 = (bf16[256,1024]{1,0:T(8,128)(2,1)}, f32[2048,256]{1,0:T(8,128)}, f32[256,1]{1,0:T(8,128)}, s32[2]{0:T(128)}) custom-call(s32[8]{0:T(128)} %counts_ref.1, bf16[256,1024]{1,0:T(8,128)(2,1)} %bitcast.42, f32[1,1024]{1,0:T(1,128)} %bitcast.44), custom_call_target="tpu_custom_call" | custom-call | tf_op jit(solution)/shard_map/prepare_rows/pallas_call | solution.py:240
  8.6 1.0 fusion.12
  9.7 38.2 %gather_rows.1 = (bf16[256,1024]{1,0:T(8,128)(2,1)}, bf16[2048,1024]{1,0:T(8,128)(2,1)}, bf16[2048,1024]{1,0:T(8,128)(2,1)}) custom-call(bf16[256,1024]{1,0:T(8,128)(2,1)} %get-tuple-element.16.normed_ref, bf16[1024,1024]{1,0:T(8,128)(2,1)} %wq_ref.1, bf16[1024,1024]{1,0:T(8,128)(2,1)} %wk_ref.3, bf16[1024,1024]{1,0:T(8,128)(2,1)} %wv_ref.3), custom_call_target="tpu_custom_call" | custom-call | tf_op jit(solution)/shard_map/gather_rows/pallas_call | solution.py:325
  47.9 0.0 copy-start.1
  47.9 33.0 %attention_forward.1 = (f32[256,1024]{1,0:T(8,128)}, f32[8,2,256]{2,1,0:T(2,128)}) custom-call(s32[2]{0:T(128)} %get-tuple-element.15.reach_ref, bf16[256,1024]{1,0:T(8,128)(2,1)} %get-tuple-element.17.q_ref, bf16[2048,1024]{1,0:T(8,128)(2,1)} %get-tuple-element.18.k_ref, bf16[2048,1024]{1,0:T(8,128)(2,1)} %get-tuple-element.19.v_ref, ...), custom_call_target="tpu_custom_call" | custom-call | tf_op jit(solution)/shard_map/attention_forward/pallas_call | solution.py:117
  80.9 0.0 copy-done
  80.9 0.0 copy-done.1
  80.9 0.0 copy-start.4
  80.9 0.0 copy-start.7
  80.9 2.1 %multiply_reduce_fusion.1 = (f32[256]{0:T(256)S(1)}, f32[256,1024]{1,0:T(8,128)S(1)}) fusion(bf16[1024,1024]{1,0:T(8,128)(2,1)S(1)} %copy-done, f32[256,1024]{1,0:T(8,128)} %get-tuple-element.21.mixed_ref, bf16[1,256,1024]{2,1,0:T(8,128)(2,1)S(1)} %copy-done.1), kind=kOutput, calls=%fused_computation.16 | convolution fusion | flops 538181376 | bytes 4719616 | tf_op jit(solution)/shard_map/dot_general | solution.py:672
  83.0 0.0 copy-start.5
  83.0 0.0 copy-done.4
  83.1 0.0 copy-done.7
  83.1 1.0 convolution_convert_fusion.1.own_ref
  84.0 8.1 %exchange_members.1 = bf16[3,256,128]{2,1,0:T(8,128)(2,1)} custom-call(bf16[256,128]{1,0:T(8,128)(2,1)} %convolution_convert_fusion.1.own_ref), custom_call_target="tpu_custom_call" | custom-call | tf_op jit(solution)/shard_map/exchange_members/pallas_call | solution.py:372
  92.2 1.0 convert_element_type.44
  93.1 0.0 copy-done.5
  93.1 1.7 multiply_reduce_fusion.2
  94.9 0.4 fusion.11
  95.3 1.5 concatenate.3.head_ref
  96.8 0.4 multiply_reduce_fusion
  97.2 1.6 convolution_convert_fusion.up_ref
  98.8 73.3 %attention_backward.1 = (bf16[256,1024]{1,0:T(8,128)(2,1)}, f32[256,1024]{1,0:T(8,128)}, f32[136,128]{1,0:T(8,128)}) custom-call(bf16[256,1024]{1,0:T(8,128)(2,1)} %get-tuple-element.17.q_ref, bf16[2048,1024]{1,0:T(8,128)(2,1)} %get-tuple-element.18.k_ref, bf16[2048,1024]{1,0:T(8,128)(2,1)} %get-tuple-element.19.v_ref, ...), custom_call_target="tpu_custom_call" | custom-call | tf_op jit(solution)/shard_map/attention_backward/pallas_call | solution.py:586
  172.1 1.2 slice.19
  173.3 0.0 copy-done.8
  173.3 2.3 %fusion.5 = (f32[256]{0:T(256)S(1)}, f32[256,1024]{1,0:T(8,128)S(1)}) fusion(bf16[1,256,1024]{2,1,0:T(8,128)(2,1)S(1)} %copy-done.2, f32[1024]{0:T(1024)S(1)} %copy-done.8, f32[256,1024]{1,0:T(8,128)} %get-tuple-element.25, bf16[256,1024]{1,0:T(8,128)(2,1)} %get-tuple-element.24, bf16[1024,1024]{1,0:T(8,128)(2,1)S(1)} %copy-done.3), kind=kOutput, calls=%fused_computation.12 | convolution fusion | flops 538181376 | bytes 5248000 | tf_op jit(solution)/shard_map/dot_general | solution.py:37
  175.6 1.2 fusion.6
  176.8 0.6 slice.18
  (10 shorter events, 0.0 us)
Async XLA Ops:
  0.6 80.3 %copy-start = (bf16[1024,1024]{1,0:T(8,128)(2,1)S(1)}, bf16[1024,1024]{1,0:T(8,128)(2,1)}, u32[]{:S(2)}) copy-start(bf16[1024,1024]{1,0:T(8,128)(2,1)} %param.19) | copy-start | bytes 6291460
  47.9 33.0 %copy-start.1 = (bf16[1,256,1024]{2,1,0:T(8,128)(2,1)S(1)}, bf16[1,256,1024]{2,1,0:T(8,128)(2,1)}, u32[]{:S(2)}) copy-start(bf16[1,256,1024]{2,1,0:T(8,128)(2,1)} %param.11) | copy-start | bytes 1572868
  80.9 2.1 %copy-start.4 = (bf16[1024,128]{1,0:T(8,128)(2,1)S(1)}, bf16[1024,128]{1,0:T(8,128)(2,1)}, u32[]{:S(2)}) copy-start(bf16[1024,128]{1,0:T(8,128)(2,1)} %param.21) | copy-start | bytes 786436
  80.9 2.1 %copy-start.7 = (f32[1024]{0:T(1024)S(1)}, f32[1024]{0:T(1024)}, u32[]{:S(2)}) copy-start(f32[1024]{0:T(1024)} %param.20) | copy-start | bytes 12292
  83.0 10.1 %copy-start.5 = (bf16[256,128]{1,0:T(8,128)(2,1)S(1)}, bf16[256,128]{1,0:T(8,128)(2,1)}, u32[]{:S(2)}) copy-start(bf16[256,128]{1,0:T(8,128)(2,1)} %param.12) | copy-start | bytes 196612
  98.8 74.5 %copy-start.2 = (bf16[1,256,1024]{2,1,0:T(8,128)(2,1)S(1)}, bf16[1,256,1024]{2,1,0:T(8,128)(2,1)}, u32[]{:S(2)}) copy-start(bf16[1,256,1024]{2,1,0:T(8,128)(2,1)} %param.11) | copy-start | bytes 1572868
  98.8 74.5 %copy-start.3 = (bf16[1024,1024]{1,0:T(8,128)(2,1)S(1)}, bf16[1024,1024]{1,0:T(8,128)(2,1)}, u32[]{:S(2)}) copy-start(bf16[1024,1024]{1,0:T(8,128)(2,1)} %wq_ref.1) | copy-start | bytes 6291460
  98.8 74.5 %copy-start.8 = (f32[1024]{0:T(1024)S(1)}, f32[1024]{0:T(1024)}, u32[]{:S(2)}) copy-start(f32[1024]{0:T(1024)} %param.15) | copy-start | bytes 12292
  175.6 1.2 copy-start.6

commit v5 on v4

--- a/solution.py
+++ b/solution.py
@@ -222,7 +222,16 @@
 
 
 def prepare_kernel(
-    bands, window, counts_ref, latent_ref, gain_ref, normed_ref, bias_ref, inverse_ref, reach_ref
+    bands,
+    window,
+    counts_ref,
+    latent_ref,
+    gain_ref,
+    normed_ref,
+    bias_ref,
+    inverse_ref,
+    share_ref,
+    reach_ref,
 ):
     band = lax.axis_index("band")
     first = jnp.clip(band - HOPS, 0, bands - window)
@@ -230,6 +239,12 @@
     inverse = inverse_rms(latent)
     inverse_ref[...] = inverse
     normed_ref[...] = (latent * inverse * gain_ref[...]).astype(jnp.bfloat16)
+    total = counts_ref[0]
+    for b in range(1, bands):
+        total += counts_ref[b]
+    slot = lax.broadcasted_iota(jnp.int32, share_ref.shape, 0)
+    all_points = jnp.full(share_ref.shape, total, jnp.int32).astype(jnp.float32) * CH
+    share_ref[...] = jnp.where(slot < counts_ref[band], 1.0, 0.0) / all_points
     write_mask(bands, window, band, first, latent.shape[0], counts_ref, bias_ref, reach_ref)
 
 
@@ -240,10 +255,11 @@
     return pl.pallas_call(
         functools.partial(prepare_kernel, bands, window),
         in_specs=[smem, vmem, vmem],
-        out_specs=[vmem, vmem, vmem, smem],
+        out_specs=[vmem, vmem, vmem, vmem, smem],
         out_shape=[
             jax.ShapeDtypeStruct((slots, model_width), jnp.bfloat16),
             jax.ShapeDtypeStruct((window * slots, slots), jnp.float32),
+            jax.ShapeDtypeStruct((slots, 1), jnp.float32),
             jax.ShapeDtypeStruct((slots, 1), jnp.float32),
             jax.ShapeDtypeStruct((2,), jnp.int32),
         ],
@@ -652,7 +668,6 @@
     gain_head,
     w_head,
 ):
-    band = lax.axis_index("band")
     bands = lax.axis_size("band")
     members = lax.axis_size("member")
     _, slots, model_width = latent.shape
@@ -660,14 +675,12 @@
     window = min(bands, 2 * HOPS + 1)
 
     latent_f = latent[0].astype(jnp.float32)
-    normed, bias, inverse_one, reach = prepare_rows(
+    normed, bias, inverse_one, share, reach = prepare_rows(
         band_counts, latent[0], gain_attn[None], bands, window
     )
     queries, key_rows, value_rows = gather_and_project(
         normed, w_query, w_key, w_value, bands, window
     )
-    own_live = jnp.arange(slots, dtype=jnp.int32) < band_counts[band]
-
     mixed, lse = attention_forward(queries, key_rows, value_rows, bias, reach)
     hidden = latent_f + jnp.dot(
         mixed.astype(jnp.bfloat16), w_out, preferred_element_type=jnp.float32
@@ -676,13 +689,11 @@
     head_in = (hidden * inverse_two * gain_head).astype(jnp.bfloat16)
     predicted = jnp.dot(head_in, w_head, preferred_element_type=jnp.float32).astype(jnp.bfloat16)
     others = exchange_members(predicted, members)
-    total_live = jnp.sum(band_counts).astype(jnp.float32) * CH
-    point_weight = area_weight * own_live.astype(jnp.float32) / total_live
     loss_part, gradient = own_accuracy(
         predicted.astype(jnp.float32),
         others.astype(jnp.float32),
         observed.astype(jnp.float32),
-        point_weight[:, None],
+        area_weight[:, None] * share,
     )
     grad_pred = gradient.astype(jnp.bfloat16)
     grad_hidden = norm_backward(hidden, gain_head, inverse_two, times_transposed(grad_pred, w_head))

time: 176 us -> 173 us (0.983)
  other arithmetic: 7.75 us -> 5.07 us
where the time goes in v5:
time: 173 us; the launch traced here: 174 us
  Pallas kernels  156 us (90%)
  matrix products  7.73 us (4%)
  other arithmetic  5.07 us (3%)
  local copies, waits for them, and re-layouts  4.37 us (3%)
    pallas_call x1, Pallas kernels, attention_backward(): pl.pallas_call(functools.partial(backward_kernel, bands, members, head_si...  73.3 us
    pallas_call x1, Pallas kernels, gather_and_project(): pl.pallas_call(functools.partial(gather_kernel, bands, window), in_specs=...  38.2 us
    pallas_call x1, Pallas kernels, attention_forward(): pl.pallas_call(functools.partial(forward_kernel, head_size, rows), grid=(...  33 us
    pallas_call x1, Pallas kernels, exchange_members(): pl.pallas_call(functools.partial(exchange_kernel, members), in_specs=[vme...  8.12 us
    dot_general x3, matrix products, times_transposed(): lax.dot_general(left_side, scaling_coefficient, (((left_side.ndim - 1,),...  4.26 us

profile of v5, /device:TPU:3, one launch (start us, length us, event | category | flops | bytes accessed | tf_op | source)
XLA Modules:
  0.0 174.0 jit_solution(7501003627761907008)
XLA Ops:
  0.6 0.0 copy-start
  0.6 1.0 copy.14
  1.6 3.4 %prepare_rows.1 = (bf16[256,1024]{1,0:T(8,128)(2,1)}, f32[2048,256]{1,0:T(8,128)}, f32[256,1]{1,0:T(8,128)}, f32[256,1]{1,0:T(8,128)}, s32[2]{0:T(128)}) custom-call(s32[8]{0:T(128)} %counts_ref.1, bf16[256,1024]{1,0:T(8,128)(2,1)} %bitcast.42, f32[1,1024]{1,0:T(1,128)} %bitcast.44), custom_call_target="tpu_custom_call" | custom-call | tf_op jit(solution)/shard_map/prepare_rows/pallas_call | solution.py:255
  5.0 1.1 fusion.11
  6.2 38.2 %gather_rows.1 = (bf16[256,1024]{1,0:T(8,128)(2,1)}, bf16[2048,1024]{1,0:T(8,128)(2,1)}, bf16[2048,1024]{1,0:T(8,128)(2,1)}) custom-call(bf16[256,1024]{1,0:T(8,128)(2,1)} %get-tuple-element.17.normed_ref, bf16[1024,1024]{1,0:T(8,128)(2,1)} %wq_ref.1, bf16[1024,1024]{1,0:T(8,128)(2,1)} %wk_ref.3, bf16[1024,1024]{1,0:T(8,128)(2,1)} %wv_ref.3), custom_call_target="tpu_custom_call" | custom-call | tf_op jit(solution)/shard_map/gather_rows/pallas_call | solution.py:341
  44.4 0.0 copy-start.1
  44.4 33.0 %attention_forward.1 = (f32[256,1024]{1,0:T(8,128)}, f32[8,2,256]{2,1,0:T(2,128)}) custom-call(s32[2]{0:T(128)} %get-tuple-element.16.reach_ref, bf16[256,1024]{1,0:T(8,128)(2,1)} %get-tuple-element.18.q_ref, bf16[2048,1024]{1,0:T(8,128)(2,1)} %get-tuple-element.19.k_ref, bf16[2048,1024]{1,0:T(8,128)(2,1)} %get-tuple-element.20.v_ref, ...), custom_call_target="tpu_custom_call" | custom-call | tf_op jit(solution)/shard_map/attention_forward/pallas_call | solution.py:117
  77.4 0.0 copy-done
  77.4 0.0 copy-done.1
  77.4 0.0 copy-start.4
  77.4 0.0 copy-start.7
  77.4 2.1 %multiply_reduce_fusion.1 = (f32[256]{0:T(256)S(1)}, f32[256,1024]{1,0:T(8,128)S(1)}) fusion(bf16[1024,1024]{1,0:T(8,128)(2,1)S(1)} %copy-done, f32[256,1024]{1,0:T(8,128)} %get-tuple-element.22.mixed_ref, bf16[1,256,1024]{2,1,0:T(8,128)(2,1)S(1)} %copy-done.1), kind=kOutput, calls=%fused_computation.16 | convolution fusion | flops 538181376 | bytes 4719616 | tf_op jit(solution)/shard_map/dot_general | solution.py:685
  79.5 0.0 copy-start.5
  79.5 0.0 copy-done.4
  79.5 0.0 copy-done.7
  79.5 1.0 convolution_convert_fusion.1.own_ref
  80.5 8.1 %exchange_members.1 = bf16[3,256,128]{2,1,0:T(8,128)(2,1)} custom-call(bf16[256,128]{1,0:T(8,128)(2,1)} %convolution_convert_fusion.1.own_ref), custom_call_target="tpu_custom_call" | custom-call | tf_op jit(solution)/shard_map/exchange_members/pallas_call | solution.py:388
  88.7 1.0 convert_element_type.39
  89.6 0.0 copy-done.5
  89.6 1.7 multiply_reduce_fusion.2
  91.3 0.4 fusion.10
  91.8 1.5 concatenate.3.head_ref
  93.3 0.4 multiply_reduce_fusion
  93.7 1.6 convolution_convert_fusion.up_ref
  95.3 73.3 %attention_backward.1 = (bf16[256,1024]{1,0:T(8,128)(2,1)}, f32[256,1024]{1,0:T(8,128)}, f32[136,128]{1,0:T(8,128)}) custom-call(bf16[256,1024]{1,0:T(8,128)(2,1)} %get-tuple-element.18.q_ref, bf16[2048,1024]{1,0:T(8,128)(2,1)} %get-tuple-element.19.k_ref, bf16[2048,1024]{1,0:T(8,128)(2,1)} %get-tuple-element.20.v_ref, ...), custom_call_target="tpu_custom_call" | custom-call | tf_op jit(solution)/shard_map/attention_backward/pallas_call | solution.py:602
  168.6 1.2 slice.19
  169.8 0.0 copy-done.2
  169.8 0.0 copy-done.3
  169.8 2.3 %fusion.5 = (f32[256]{0:T(256)S(1)}, f32[256,1024]{1,0:T(8,128)S(1)}) fusion(bf16[1,256,1024]{2,1,0:T(8,128)(2,1)S(1)} %copy-done.2, f32[1024]{0:T(1024)S(1)} %copy-done.8, f32[256,1024]{1,0:T(8,128)} %get-tuple-element.27, bf16[256,1024]{1,0:T(8,128)(2,1)} %get-tuple-element.26, bf16[1024,1024]{1,0:T(8,128)(2,1)S(1)} %copy-done.3), kind=kOutput, calls=%fused_computation.12 | convolution fusion | flops 538181376 | bytes 5248000 | tf_op jit(solution)/shard_map/dot_general | solution.py:37
  172.1 1.2 fusion.6
  173.3 0.0 copy-done.6
  173.3 0.6 slice.18
  (8 shorter events, 0.0 us)
Async XLA Ops:
  0.6 76.8 %copy-start = (bf16[1024,1024]{1,0:T(8,128)(2,1)S(1)}, bf16[1024,1024]{1,0:T(8,128)(2,1)}, u32[]{:S(2)}) copy-start(bf16[1024,1024]{1,0:T(8,128)(2,1)} %param.19) | copy-start | bytes 6291460
  44.4 33.0 %copy-start.1 = (bf16[1,256,1024]{2,1,0:T(8,128)(2,1)S(1)}, bf16[1,256,1024]{2,1,0:T(8,128)(2,1)}, u32[]{:S(2)}) copy-start(bf16[1,256,1024]{2,1,0:T(8,128)(2,1)} %param.11) | copy-start | bytes 1572868
  77.4 2.1 %copy-start.4 = (bf16[1024,128]{1,0:T(8,128)(2,1)S(1)}, bf16[1024,128]{1,0:T(8,128)(2,1)}, u32[]{:S(2)}) copy-start(bf16[1024,128]{1,0:T(8,128)(2,1)} %param.21) | copy-start | bytes 786436
  77.4 2.1 %copy-start.7 = (f32[1024]{0:T(1024)S(1)}, f32[1024]{0:T(1024)}, u32[]{:S(2)}) copy-start(f32[1024]{0:T(1024)} %param.20) | copy-start | bytes 12292
  79.5 10.1 %copy-start.5 = (bf16[256,128]{1,0:T(8,128)(2,1)S(1)}, bf16[256,128]{1,0:T(8,128)(2,1)}, u32[]{:S(2)}) copy-start(bf16[256,128]{1,0:T(8,128)(2,1)} %param.12) | copy-start | bytes 196612
  95.3 74.5 %copy-start.2 = (bf16[1,256,1024]{2,1,0:T(8,128)(2,1)S(1)}, bf16[1,256,1024]{2,1,0:T(8,128)(2,1)}, u32[]{:S(2)}) copy-start(bf16[1,256,1024]{2,1,0:T(8,128)(2,1)} %param.11) | copy-start | bytes 1572868
  95.3 74.5 %copy-start.3 = (bf16[1024,1024]{1,0:T(8,128)(2,1)S(1)}, bf16[1024,1024]{1,0:T(8,128)(2,1)}, u32[]{:S(2)}) copy-start(bf16[1024,1024]{1,0:T(8,128)(2,1)} %wq_ref.1) | copy-start | bytes 6291460
  95.3 74.5 %copy-start.8 = (f32[1024]{0:T(1024)S(1)}, f32[1024]{0:T(1024)}, u32[]{:S(2)}) copy-start(f32[1024]{0:T(1024)} %param.15) | copy-start | bytes 12292
  172.1 1.2 copy-start.6
